TPU v7x, 32 devices: a whole 2x2x4 slice. The times are simulated.
32 devices in a mesh: dp: 2 (over x), mp: 16 (over z, y, core).
Axes of the slice: x: 2, y: 2, z: 4, core: 2. Of those that a mesh axis runs over, the one named last changes fastest.
Arguments:
- inputs: bfloat16 [1024, 4608], P(('dp', 'mp')), may hold values from -6 to 6
- lengths: int32 [2], P('dp'), may hold values from 1 to 512, as said below
- gain_in: float32 [4608], replicated, may hold values from 0.1 to 1.9
- query_weight: float32 [4608, 4096], P('dp', 'mp'), may hold values from -0.11785113 to 0.11785113
- key_weight: float32 [4608, 2048], P('dp', 'mp'), may hold values from -0.11785113 to 0.11785113
- value_weight: float32 [4608, 2048], P('dp', 'mp'), may hold values from -0.09375 to 0.09375
- output_weight: bfloat16 [4096, 4608], P('mp'), may hold values from -0.09375 to 0.09375
- gain_post: float32 [4608], replicated, may hold values from 0.1 to 1.9
- gain_pre: float32 [4608], replicated, may hold values from 0.1 to 1.9
- gate_weight: float32 [4608, 20480], P('dp', 'mp'), may hold values from -0.09375 to 0.09375
- up_weight: float32 [4608, 20480], P('dp', 'mp'), may hold values from -0.09375 to 0.09375
Outputs:
- residual: bfloat16 [1024, 4608], P(('dp', 'mp'))
- hidden: bfloat16 [1024, 20480], P('dp', 'mp')
- keys_out: bfloat16 [1024, 2048], P('dp', 'mp')
- values_out: bfloat16 [1024, 2048], P('dp', 'mp')
Inputs may be any that keep to these rules, and one draw needn't show every extreme that they name: Half of the 2 prompts have lengths under 512 // 16, the others at least 448; at least one prompt fills its slot.
All inputs are finite; a program needn't handle non-finite values.
Results may differ from a plain program's by a relative error of at most 0.03.
Values may be sent and summed in bfloat16 or wider, within the bound.
A program may use at most 128 MiB of HBM per device.

v0:
```python
import math

import jax
import jax.numpy as jnp
from jax import lax
from jax.sharding import PartitionSpec as P

KVH = 16


query_scale = 1.0 / 12.0
soft_cap = 50.0


def swapped(value, axis, stride):
    mask = 2**stride
    pairs = [(source, source ^ mask) for source in range(lax.axis_size(axis))]
    return lax.ppermute(value, axis, pairs)


def rms_norm(values, gain):
    mean_sq = jnp.mean(values * values, axis=-1, keepdims=True)
    return values * lax.rsqrt(mean_sq + 1e-06) * gain


def rotate_pairs(values, positions):
    half_size = values.shape[-1] // 2
    freqs = jnp.exp(
        jnp.arange(half_size, dtype=jnp.float32) * (-2.0 * math.log(10000.0) / values.shape[-1])
    )
    angles = positions.astype(jnp.float32)[:, None] * freqs[None, :]
    cosine = jnp.cos(angles)[:, None, :]
    sine = jnp.sin(angles)[:, None, :]
    first = values[..., :half_size]
    second = values[..., half_size:]
    return jnp.concatenate(
        [first * cosine - second * sine, second * cosine + first * sine], axis=-1
    )


def join_halves(own_half, other_half, odd_flag):
    lower_first = jnp.concatenate([own_half, other_half], axis=1)
    upper_first = jnp.concatenate([other_half, own_half], axis=1)
    return jnp.where(odd_flag, upper_first, lower_first)


def head_block(query_rows, key_rows, value_rows, key_count, length):
    scores = (
        jnp.einsum("qhd,kd->hqk", query_rows, key_rows, preferred_element_type=jnp.float32)
        * query_scale
    )
    capped = soft_cap * jnp.tanh(scores / soft_cap)
    query_pos = jnp.arange(query_rows.shape[0], dtype=jnp.int32)
    key_pos = jnp.arange(key_count, dtype=jnp.int32)
    allowed = (key_pos[None, :] <= query_pos[:, None]) & (key_pos[None, :] < length)
    weights_exp = jnp.where(allowed[None], jnp.exp(capped), jnp.float32(0.0))
    probs = (weights_exp / jnp.sum(weights_exp, axis=-1, keepdims=True)).astype(jnp.bfloat16)
    return jnp.einsum("hqk,kd->qhd", probs, value_rows, preferred_element_type=jnp.float32)


def on_device(
    inputs,
    lengths,
    gain_in,
    query_weight,
    key_weight,
    value_weight,
    output_weight,
    gain_post,
    gain_pre,
    gate_weight,
    up_weight,
):
    mp_count = lax.axis_size("mp")
    mp_index = lax.axis_index("mp")
    odd_flag = mp_index % 2 == 1
    paired = mp_count > KVH
    gate_bf = gate_weight.astype(jnp.bfloat16)
    up_bf = up_weight.astype(jnp.bfloat16)
    normed_local = rms_norm(inputs.astype(jnp.float32), gain_in).astype(jnp.bfloat16)
    normed = lax.all_gather(normed_local, "mp", axis=0, tiled=True)
    group_tokens = normed.shape[0]
    prompts = lengths.shape[0]
    slot = group_tokens // prompts
    query_bf = query_weight.astype(jnp.bfloat16)
    key_bf = key_weight.astype(jnp.bfloat16)
    value_bf = value_weight.astype(jnp.bfloat16)
    own_width = key_weight.shape[1]
    if paired:
        other_key, other_value = swapped((key_bf, value_bf), "mp", 0)
        key_bf = join_halves(key_bf, other_key, odd_flag)
        value_bf = join_halves(value_bf, other_value, odd_flag)
    pieces = (
        lax.all_gather(query_bf, "dp", axis=0, tiled=True),
        lax.all_gather(key_bf, "dp", axis=0, tiled=True),
        lax.all_gather(value_bf, "dp", axis=0, tiled=True),
    )
    columns = normed
    raw_q, raw_k, raw_v = tuple(
        (jnp.dot(columns, piece, preferred_element_type=jnp.float32) for piece in pieces)
    )
    head_size = raw_k.shape[1]
    local_heads = raw_q.shape[1] // head_size
    positions = jnp.arange(group_tokens, dtype=jnp.int32) % slot
    row_len = jnp.repeat(lengths, slot, total_repeat_length=group_tokens)
    live = positions < row_len
    queries = rotate_pairs(raw_q.reshape(group_tokens, local_heads, head_size), positions).astype(
        jnp.bfloat16
    )
    keys_rot = rotate_pairs(raw_k.reshape(group_tokens, 1, head_size), positions).reshape(
        group_tokens, head_size
    )
    keys_rot = jnp.where(live[:, None], keys_rot, jnp.float32(0.0)).astype(jnp.bfloat16)
    values_all = jnp.where(live[:, None], raw_v, jnp.float32(0.0)).astype(jnp.bfloat16)
    key_rows = keys_rot[0:slot]
    value_rows = values_all[0:slot]
    length = lengths[0]
    mixed = head_block(queries, key_rows, value_rows, slot, length)
    slot_pos = jnp.arange(slot, dtype=jnp.int32)
    mixed = jnp.where((slot_pos < length)[:, None, None], mixed, jnp.float32(0.0))
    attended_list = mixed.astype(jnp.bfloat16).reshape(slot, local_heads * head_size)
    attn_rows = lax.psum_scatter(
        jnp.dot(attended_list, output_weight, preferred_element_type=jnp.float32).astype(
            jnp.bfloat16
        ),
        "mp",
        scatter_dimension=0,
        tiled=True,
    ).astype(jnp.float32)
    residual = (inputs.astype(jnp.float32) + rms_norm(attn_rows, gain_post)).astype(jnp.bfloat16)
    pre_local = rms_norm(residual.astype(jnp.float32), gain_pre).astype(jnp.bfloat16)
    pre_ffn = lax.all_gather(pre_local, "mp", axis=0, tiled=True)
    pieces = (
        lax.all_gather(gate_bf, "dp", axis=0, tiled=True),
        lax.all_gather(up_bf, "dp", axis=0, tiled=True),
    )
    columns = pre_ffn
    gate = jnp.dot(columns, pieces[0], preferred_element_type=jnp.float32)
    up_part = jnp.dot(columns, pieces[1], preferred_element_type=jnp.float32)
    hidden = (jax.nn.gelu(gate, approximate=True) * up_part).astype(jnp.bfloat16)
    if paired:
        offset = mp_index % 2 * own_width
        keys_out = lax.dynamic_slice_in_dim(keys_rot, offset, own_width, 1)
        values_out = lax.dynamic_slice_in_dim(values_all, offset, own_width, 1)
    else:
        keys_out = keys_rot
        values_out = values_all
    return (residual, hidden, keys_out, values_out)


def solution(mesh):
    in_specs = (
        P(("dp", "mp"), None),
        P("dp"),
        P(),
        P("dp", "mp"),
        P("dp", "mp"),
        P("dp", "mp"),
        P("mp", None),
        P(),
        P(),
        P("dp", "mp"),
        P("dp", "mp"),
    )
    out_specs = (P(("dp", "mp"), None), P("dp", "mp"), P("dp", "mp"), P("dp", "mp"))
    return jax.shard_map(
        on_device, mesh=mesh, in_specs=in_specs, out_specs=out_specs, check_vma=False
    )
```

profile of v0, /device:TPU:0, one launch (start us, length us, event | category | flops | bytes accessed | tf_op | source)
XLA Modules:
  0.0 603.5 jit_solution(9777329664425042141)
XLA Ops:
  7.2 0.0 all-gather.12.cloned.1.call-start
  7.3 2.3 convert_element_type.82
  9.6 0.0 all-gather.12.cloned.1.call-update
  9.6 0.0 all-gather.8.cloned.1.call-start
  9.7 1.1 fusion.17
  10.8 0.9 fusion.19
  11.7 0.0 all-gather.8.cloned.1.call-update
  11.7 0.0 all-gather.14.cloned.1.call-start
  11.7 2.8 convert_element_type.85
  14.5 0.0 all-gather.14.cloned.1.call-update
  14.6 0.0 all-gather.10.cloned.1.call-start
  14.6 2.1 convert_element_type.80
  16.8 0.0 all-gather.10.cloned.1.call-update
  16.8 0.0 reduce-scatter.2.cloned.1.call-start
  17.5 0.9 fusion.11
  18.4 1.8 multiply_cosine_fusion
  20.2 15.1 %all-gather.12.cloned.1.call-done = bf16[4608,128]{1,0:T(8,128)(2,1)} async-done(((bf16[2304,128]{1,0:T(8,128)(2,1)}), bf16[4608,128]{1,0:T(8,128)(2,1)}) %all-gather.12.cloned.1.call-update) | async-done | bytes 1179664 | tf_op jit(solution)/shard_map/all_gather | solution.py:95
  35.2 56.3 %all-gather.8.cloned.1.call-done = bf16[512,4608]{1,0:T(8,128)(2,1)} async-done(((bf16[32,4608]{1,0:T(8,128)(2,1)}), bf16[512,4608]{1,0:T(8,128)(2,1)}) %all-gather.8.cloned.1.call-update) | async-done | bytes 4718608 | tf_op jit(solution)/shard_map/all_gather | solution.py:81
  91.5 4.1 convolution_bitcast_fusion
  95.6 32.7 %all-gather.14.cloned.1.call-done = bf16[4608,256]{1,0:T(8,128)(2,1)} async-done(((bf16[2304,256]{1,0:T(8,128)(2,1)}), bf16[4608,256]{1,0:T(8,128)(2,1)}) %all-gather.14.cloned.1.call-update) | async-done | bytes 2359312 | tf_op jit(solution)/shard_map/all_gather | solution.py:94
  128.3 4.5 fusion.43
  132.8 0.8 fusion.42
  133.7 1.1 copy.25
  134.8 2.0 copy.24
  136.8 1.2 fusion.25
  138.0 0.2 fusion.28
  138.2 1.4 subtract_convert_fusion
  139.6 2.2 bitcast_select_fusion
  141.8 10.7 %all-gather.10.cloned.1.call-done = bf16[4608,128]{1,0:T(8,128)(2,1)} async-done(((bf16[2304,128]{1,0:T(8,128)(2,1)}), bf16[4608,128]{1,0:T(8,128)(2,1)}) %all-gather.10.cloned.1.call-update) | async-done | bytes 1179664 | tf_op jit(solution)/shard_map/all_gather | solution.py:96
  152.5 4.1 fusion.9
  156.6 2.7 fusion.8
  159.4 3.5 convolution_convert_fusion
  162.9 0.0 reduce-scatter.2.cloned.1.call-update
  162.9 0.0 all-gather.18.cloned.1.call-start
  163.0 7.4 %convert_element_type.94 = bf16[2304,1280]{1,0:T(8,128)(2,1)} convert(f32[2304,1280]{1,0:T(8,128)} %param.24) | non-fusion elementwise | flops 2949120 | bytes 17694720 | tf_op jit(solution)/shard_map/convert_element_type | solution.py:78
  170.4 0.0 all-gather.16.cloned.1.call-start
  170.5 68.1 %reduce-scatter.2.cloned.1.call-done = bf16[32,4608]{1,0:T(8,128)(2,1)} async-done(((bf16[512,4608]{1,0:T(8,128)(2,1)}), bf16[32,4608]{1,0:T(8,128)(2,1)}) %reduce-scatter.2.cloned.1.call-update) | async-done | bytes 294928 | tf_op jit(solution)/shard_map/reduce_scatter | solution.py:122
  238.6 1.1 fusion.12
  239.7 1.3 fusion.14
  241.1 0.9 fusion.16
  241.9 0.2 all-gather.20.cloned.1.call-start
  242.2 9.5 %convert_element_type.95 = bf16[2304,1280]{1,0:T(8,128)(2,1)} convert(f32[2304,1280]{1,0:T(8,128)} %param.25) | non-fusion elementwise | flops 2949120 | bytes 17694720 | tf_op jit(solution)/shard_map/convert_element_type | solution.py:79
  251.7 0.0 all-gather.20.cloned.1.call-update
  251.7 131.3 %all-gather.18.cloned.1.call-done = bf16[4608,1280]{1,0:T(8,128)(2,1)} async-done(((bf16[2304,1280]{1,0:T(8,128)(2,1)}), bf16[4608,1280]{1,0:T(8,128)(2,1)}) %all-gather.18.cloned.1.call-update) | async-done | bytes 11796496 | tf_op jit(solution)/shard_map/all_gather | solution.py:134
  383.1 56.5 %all-gather.16.cloned.1.call-done = bf16[512,4608]{1,0:T(8,128)(2,1)} async-done(((bf16[32,4608]{1,0:T(8,128)(2,1)}), bf16[512,4608]{1,0:T(8,128)(2,1)}) %all-gather.16.cloned.1.call-update) | async-done | bytes 4718608 | tf_op jit(solution)/shard_map/all_gather | solution.py:132
  439.6 12.6 %fusion.44 = f32[512,1280]{1,0:T(8,128)} fusion(bf16[512,4608]{1,0:T(8,128)(2,1)} %all-gather.16.cloned.1.call-done, bf16[4608,1280]{1,0:T(8,128)(2,1)} %all-gather.18.cloned.1.call-done), kind=kOutput, calls=%fused_computation.73 | convolution fusion | flops 6039797760 | bytes 19136512 | tf_op jit(solution)/shard_map/dot_general | solution.py:138
  452.2 131.5 %all-gather.20.cloned.1.call-done = bf16[4608,1280]{1,0:T(8,128)(2,1)} async-done(((bf16[2304,1280]{1,0:T(8,128)(2,1)}), bf16[4608,1280]{1,0:T(8,128)(2,1)}) %all-gather.20.cloned.1.call-update) | async-done | bytes 11796496 | tf_op jit(solution)/shard_map/all_gather | solution.py:135
  583.7 13.0 %fusion = bf16[512,1280]{1,0:T(8,128)(2,1)} fusion(bf16[512,4608]{1,0:T(8,128)(2,1)} %all-gather.16.cloned.1.call-done, bf16[4608,1280]{1,0:T(8,128)(2,1)} %all-gather.20.cloned.1.call-done, f32[512,1280]{1,0:T(8,128)} %fusion.44), kind=kOutput, calls=%fused_computation.3 | convolution fusion | flops 6046351360 | bytes 20447232 | tf_op jit(solution)/shard_map/dot_general | solution.py:139
  (29 shorter events, 0.1 us)
Async XLA Ops:
  7.2 152.2 %copy-start = (bf16[256,4608]{1,0:T(8,128)(2,1)S(1)}, bf16[256,4608]{1,0:T(8,128)(2,1)}, u32[]{:S(2)}) copy-start(bf16[256,4608]{1,0:T(8,128)(2,1)} %param.21) | copy-start | bytes 7077892
  7.2 3.6 copy-start.2
  7.2 3.6 copy-start.6
  7.2 28.0 %all-gather.12.cloned.1.call-start = ((), (), s32[]{:S(2)}) async-start(), calls=%async_computation.3 | async-start | bytes 1769472 | tf_op jit(solution)/shard_map/all_gather | solution.py:95
  9.6 81.9 %all-gather.8.cloned.1.call-start = ((), (), s32[]{:S(2)}) async-start(), calls=%async_computation.1 | async-start | bytes 5013504 | tf_op jit(solution)/shard_map/all_gather | solution.py:81
  11.7 116.6 %all-gather.14.cloned.1.call-start = ((), (), s32[]{:S(2)}) async-start(), calls=%async_computation.4 | async-start | bytes 3538944 | tf_op jit(solution)/shard_map/all_gather | solution.py:94
  14.6 137.9 %all-gather.10.cloned.1.call-start = ((), (), s32[]{:S(2)}) async-start(), calls=%async_computation.2 | async-start | bytes 1769472 | tf_op jit(solution)/shard_map/all_gather | solution.py:96
  16.8 221.8 %reduce-scatter.2.cloned.1.call-start = ((), (), s32[]{:S(2)}) async-start(), calls=%async_computation.5 | async-start | bytes 5013504 | tf_op jit(solution)/shard_map/reduce_scatter | solution.py:122
  136.8 2.8 copy-start.4
  138.2 1.4 copy-start.5
  156.6 2.8 copy-start.9
  162.9 220.1 %all-gather.18.cloned.1.call-start = ((), (), s32[]{:S(2)}) async-start(), calls=%async_computation.7 | async-start | bytes 17694720 | tf_op jit(solution)/shard_map/all_gather | solution.py:134
  170.4 69.3 %copy-start.8 = (f32[4608]{0:T(1024)S(1)}, f32[4608]{0:T(1024)}, u32[]{:S(2)}) copy-start(f32[4608]{0:T(1024)} %param.22) | copy-start | bytes 55300
  170.4 70.7 %copy-start.7 = (f32[4608]{0:T(1024)S(1)}, f32[4608]{0:T(1024)}, u32[]{:S(2)}) copy-start(f32[4608]{0:T(1024)} %param.23) | copy-start | bytes 55300
  170.4 269.2 %all-gather.16.cloned.1.call-start = ((), (), s32[]{:S(2)}) async-start(), calls=%async_computation.6 | async-start | bytes 5013504 | tf_op jit(solution)/shard_map/all_gather | solution.py:132
  241.0 10.7 %copy-start.3 = (bf16[32,4608]{1,0:T(8,128)(2,1)}, bf16[32,4608]{1,0:T(8,128)(2,1)S(1)}, u32[]{:S(2)}) copy-start(bf16[32,4608]{1,0:T(8,128)(2,1)S(1)} %get-tuple-element.29) | copy-start | bytes 884740
  241.9 341.8 %all-gather.20.cloned.1.call-start = ((), (), s32[]{:S(2)}) async-start(), calls=%async_computation.8 | async-start | bytes 17694720 | tf_op jit(solution)/shard_map/all_gather | solution.py:135
  583.7 13.0 %copy-start.1 = (bf16[256,4608]{1,0:T(8,128)(2,1)S(1)}, bf16[256,4608]{1,0:T(8,128)(2,1)}, u32[]{:S(2)}) copy-start(bf16[256,4608]{1,0:T(8,128)(2,1)} %param.21) | copy-start | bytes 7077892
Sparse Core Ops, SparseCore 0:
  9.7 25.4 all-gather.11
  38.1 53.3 all-gather.7
  93.6 34.6 all-gather.13
  129.7 22.7 all-gather.9
  163.0 75.5 reduce-scatter.1
  240.1 142.9 all-gather.17
  386.2 53.3 all-gather.15
  441.2 142.4 all-gather.19
where the time goes:
time: 604 us
  waiting for transfers between devices  502 us (83%)
  matrix products  46.8 us (8%)
  other arithmetic  34.9 us (6%)
  between operations  15 us (2%)
    all_gather x1, waiting for transfers between devices, on_device(): lax.all_gather(up_bf, 'dp', axis=0, tiled=True)  131 us
    all_gather x1, waiting for transfers between devices, on_device(): lax.all_gather(gate_bf, 'dp', axis=0, tiled=True)  131 us
    reduce_scatter x1, waiting for transfers between devices, on_device(): lax.psum_scatter(jnp.dot(attended_list, output_weight, preferred_element_...  68.1 us
    all_gather x1, waiting for transfers between devices, on_device(): pre_ffn = lax.all_gather(pre_local, 'mp', axis=0, tiled=True)  56.5 us
    all_gather x1, waiting for transfers between devices, on_device(): normed = lax.all_gather(normed_local, 'mp', axis=0, tiled=True)  56.3 us
    all_gather x1, waiting for transfers between devices, on_device(): lax.all_gather(query_bf, 'dp', axis=0, tiled=True)  32.7 us
    all_gather x1, waiting for transfers between devices, on_device(): lax.all_gather(key_bf, 'dp', axis=0, tiled=True)  15.1 us
    dot_general x1, matrix products, on_device(): up_part = jnp.dot(columns, pieces[1], preferred_element_type=jnp.float32)  13 us
  transfers between devices with their start and end apart: 8, of which 8 were waited for; matrix products, arithmetic and copies ran while one was open for 10% of the time, Pallas kernels for 0%

commit v1 on v0

--- a/solution.py
+++ b/solution.py
@@ -148,7 +148,111 @@
     return (residual, hidden, keys_out, values_out)
 
 
+def swap_dp(value):
+    return lax.ppermute(value, "dp", [(0, 1), (1, 0)])
+
+
+def gather_mp(block):
+    return lax.all_gather(block, "mp", axis=0, tiled=True)
+
+
+def scatter_mp(partial):
+    return lax.psum_scatter(partial, "mp", scatter_dimension=0, tiled=True)
+
+
+def split_rows(block):
+    half = block.shape[1] // 2
+    index = lax.axis_index("dp")
+    own = lax.dynamic_slice_in_dim(block, index * half, half, 1)
+    other = lax.dynamic_slice_in_dim(block, (1 - index) * half, half, 1)
+    return own, other
+
+
+def exchange_gather(block):
+    own, other = split_rows(block)
+    arrived = swap_dp(other)
+    own, arrived = lax.optimization_barrier((own, arrived))
+    partner_tokens = gather_mp(arrived)
+    own_tokens = gather_mp(own)
+    return own_tokens, partner_tokens
+
+
+def on_device_pair(
+    inputs,
+    lengths,
+    gain_in,
+    query_weight,
+    key_weight,
+    value_weight,
+    output_weight,
+    gain_post,
+    gain_pre,
+    gate_weight,
+    up_weight,
+):
+    bf16 = jnp.bfloat16
+    slot = inputs.shape[0] * lax.axis_size("mp")
+    length = lengths[0]
+    normed_local = rms_norm(inputs.astype(jnp.float32), gain_in).astype(bf16)
+    own_tokens, partner_tokens = exchange_gather(normed_local)
+    qkv_weight = jnp.concatenate([query_weight, key_weight, value_weight], axis=1).astype(bf16)
+    head_size = key_weight.shape[1]
+    local_heads = query_weight.shape[1] // head_size
+    partner_part = jnp.dot(partner_tokens, qkv_weight, preferred_element_type=jnp.float32)
+    arrived = swap_dp(partner_part.astype(bf16))
+    raw = jnp.dot(own_tokens, qkv_weight, preferred_element_type=jnp.float32)
+    raw = raw + arrived.astype(jnp.float32)
+    q_cols = local_heads * head_size
+    raw_q, raw_k, raw_v = (
+        raw[:, :q_cols],
+        raw[:, q_cols : q_cols + head_size],
+        raw[:, q_cols + head_size :],
+    )
+    positions = jnp.arange(slot, dtype=jnp.int32)
+    live = positions < length
+    queries = rotate_pairs(raw_q.reshape(slot, local_heads, head_size), positions).astype(bf16)
+    keys_rot = rotate_pairs(raw_k.reshape(slot, 1, head_size), positions).reshape(slot, head_size)
+    keys_rot = jnp.where(live[:, None], keys_rot, jnp.float32(0.0)).astype(bf16)
+    values_all = jnp.where(live[:, None], raw_v, jnp.float32(0.0)).astype(bf16)
+    mixed = head_block(queries, keys_rot, values_all, slot, length)
+    mixed = jnp.where(live[:, None, None], mixed, jnp.float32(0.0))
+    attended = mixed.astype(bf16).reshape(slot, local_heads * head_size)
+    attn_rows = scatter_mp(
+        jnp.dot(attended, output_weight, preferred_element_type=jnp.float32).astype(bf16)
+    ).astype(jnp.float32)
+    residual = (inputs.astype(jnp.float32) + rms_norm(attn_rows, gain_post)).astype(bf16)
+    pre_local = rms_norm(residual.astype(jnp.float32), gain_pre).astype(bf16)
+    own_tokens, partner_tokens = exchange_gather(pre_local)
+    columns = gate_weight.shape[1]
+    width = 256
+    weights = []
+    sent = []
+    for start in range(0, columns, width):
+        pair = tuple(
+            weight[:, start : start + width].astype(bf16) for weight in (gate_weight, up_weight)
+        )
+        weights.append(pair)
+        sent.append(
+            tuple(
+                swap_dp(
+                    jnp.dot(partner_tokens, piece, preferred_element_type=jnp.float32).astype(bf16)
+                )
+                for piece in pair
+            )
+        )
+    hidden = []
+    for pair, arrived in zip(weights, sent):
+        gate, up_part = tuple(
+            jnp.dot(own_tokens, piece, preferred_element_type=jnp.float32)
+            + other.astype(jnp.float32)
+            for piece, other in zip(pair, arrived)
+        )
+        hidden.append((jax.nn.gelu(gate, approximate=True) * up_part).astype(bf16))
+    return (residual, jnp.concatenate(hidden, axis=1), keys_rot, values_all)
+
+
 def solution(mesh):
+    pair_form = mesh.shape["dp"] == 2 and mesh.shape["mp"] <= KVH
     in_specs = (
         P(("dp", "mp"), None),
         P("dp"),
@@ -164,5 +268,5 @@
     )
     out_specs = (P(("dp", "mp"), None), P("dp", "mp"), P("dp", "mp"), P("dp", "mp"))
     return jax.shard_map(
-        on_device, mesh=mesh, in_specs=in_specs, out_specs=out_specs, check_vma=False
-    )
+        on_device_pair if pair_form else on_device, mesh=mesh, in_specs=in_specs, out_specs=out_specs, check_vma=False
+    )

time: 604 us -> 331 us (0.55)
  waiting for transfers between devices: 502 us -> 205 us
  starting transfers between devices: 0.51 us -> 17.7 us
  matrix products: 46.8 us -> 52.9 us
    all_gather x7 -> x4, waiting for transfers between devices: 434 us -> 105 us  [gather_mp(): return lax.all_gather(block, 'mp', axis=0, tiled=True)]
    ppermute x0 -> x13, waiting for transfers between devices: none -> 24.9 us  [swap_dp(): return lax.ppermute(value, 'dp', [(0, 1), (1, 0)])]
    convert_element_type x8 -> x3, other arithmetic: 26.1 us -> 2.29 us  [the longest x1 1.11 us: on_device_pair(): normed_local = rms_norm(inputs.astype(jnp.float32), gain_in).astype(bf16)]
    another operation x1 -> x6, other arithmetic: 1.38 us -> 21 us
    ppermute x0 -> x13, starting transfers between devices: none -> 17.3 us  [swap_dp(): return lax.ppermute(value, 'dp', [(0, 1), (1, 0)])]
    reduce_scatter x1, waiting for transfers between devices: 68.1 us -> 74.5 us  [scatter_mp(): return lax.psum_scatter(partial, 'mp', scatter_dimension=0, tiled=True)]
    dot_general x6 -> x23, matrix products: 41.8 us -> 48 us  [the longest x10 19.3 us: on_device_pair(): jnp.dot(own_tokens, piece, preferred_element_type=jnp.float32)]
  transfers between devices with their start and end apart: 8 -> 18, of which waited for: 8 -> 11; matrix products, arithmetic and copies ran while one was open for 10% -> 19% of each run, Pallas kernels for 0% -> 0%
where the time goes in v1:
time: 331 us; the launch traced here: 330 us
  waiting for transfers between devices  205 us (62%)
  matrix products  52.9 us (16%)
  other arithmetic  30.9 us (9%)
  starting transfers between devices  17.7 us (5%)
  between operations  14.8 us (4%)
  local copies, waits for them, and re-layouts  8.9 us (3%)
    all_gather x4, waiting for transfers between devices, gather_mp(): return lax.all_gather(block, 'mp', axis=0, tiled=True)  105 us
    reduce_scatter x1, waiting for transfers between devices, scatter_mp(): return lax.psum_scatter(partial, 'mp', scatter_dimension=0, tiled=True)  74.5 us
    ppermute x13, waiting for transfers between devices, swap_dp(): return lax.ppermute(value, 'dp', [(0, 1), (1, 0)])  24.9 us
    another operation x6, other arithmetic  21 us
    dot_general x10, matrix products, on_device_pair(): jnp.dot(own_tokens, piece, preferred_element_type=jnp.float32)  19.3 us
    dot_general x10, matrix products, on_device_pair(): jnp.dot(partner_tokens, piece, preferred_element_type=jnp.float32)  17.3 us
    ppermute x13, starting transfers between devices, swap_dp(): return lax.ppermute(value, 'dp', [(0, 1), (1, 0)])  17.3 us
    unnamed x57, local copies, waits for them, and re-layouts  6.71 us
  transfers between devices with their start and end apart: 18, of which 11 were waited for; matrix products, arithmetic and copies ran while one was open for 19% of the time, Pallas kernels for 0%

profile of v1, /device:TPU:0, one launch (start us, length us, event | category | flops | bytes accessed | tf_op | source)
XLA Modules:
  0.0 330.5 jit_solution(14351363262403946248)
XLA Ops:
  10.3 2.9 collective-permute-start
  13.3 3.8 %collective-permute-done = bf16[32,2304]{1,0:T(8,128)(2,1)S(1)} collective-permute-done((bf16[32,2304]{1,0:T(8,128)(2,1)S(1)}, bf16[32,2304]{1,0:T(8,128)(2,1)S(1)}, u32[]{:S(2)}, u32[]{:S(2)}) %collective-permute-start) | collective-permute-done | bytes 147488 | tf_op jit(solution)/shard_map/ppermute | solution.py:152
  18.6 1.9 convert.29
  20.5 2.1 convert.30
  24.2 37.5 %all-gather.7.cloned.1.call-done = bf16[512,2304]{1,0:T(8,128)(2,1)} async-done(((bf16[32,2304]{1,0:T(8,128)(2,1)}), bf16[512,2304]{1,0:T(8,128)(2,1)}) %all-gather.7.cloned.1.call-update) | async-done | bytes 2359312 | tf_op jit(solution)/shard_map/all_gather | solution.py:156
  61.7 4.2 %convolution_convert_fusion.1 = bf16[512,512]{0,1:T(8,128)(2,1)} fusion(bf16[512,2304]{1,0:T(8,128)(2,1)} %all-gather.7.cloned.1.call-done, bf16[2304,128]{1,0:T(8,128)(2,1)} %convert.31, bf16[2304,128]{1,0:T(8,128)(2,1)} %convert.30, bf16[2304,256]{1,0:T(8,128)(2,1)S(1)} %convert.29), kind=kOutput, calls=%fused_computation.5 | convolution fusion | flops 1215299584 | bytes 5242880 | tf_op jit(solution)/shard_map/dot_general | solution.py:201
  65.9 1.5 collective-permute-start.1
  68.2 1.8 multiply_cosine_fusion
  70.0 35.1 %all-gather.5.cloned.1.call-done = bf16[512,2304]{1,0:T(8,128)(2,1)} async-done(((bf16[32,2304]{1,0:T(8,128)(2,1)}), bf16[512,2304]{1,0:T(8,128)(2,1)}) %all-gather.5.cloned.1.call-update) | async-done | bytes 2359312 | tf_op jit(solution)/shard_map/all_gather | solution.py:156
  105.0 3.5 %convolution_add_fusion = f32[512,512]{0,1:T(8,128)S(1)} fusion(bf16[512,2304]{1,0:T(8,128)(2,1)} %all-gather.5.cloned.1.call-done, bf16[512,512]{0,1:T(8,128)(2,1)} %collective-permute-done.1, bf16[2304,128]{1,0:T(8,128)(2,1)} %convert.31, bf16[2304,128]{1,0:T(8,128)(2,1)} %convert.30, bf16[2304,256]{1,0:T(8,128)(2,1)S(1)} %convert.29), kind=kOutput, calls=%fused_computation.4 | convolution fusion | flops 1215561728 | bytes 6291456 | tf_op jit(solution)/shard_map/dot_general | solution.py:203
  114.3 2.2 bitcast_select_fusion
  116.5 2.7 fusion
  119.2 3.6 %convolution_convert_fusion = bf16[512,4608]{1,0:T(8,128)(2,1)} fusion(bf16[512,256]{0,1:T(8,128)(2,1)S(1)} %bitcast.54, bf16[256,4608]{1,0:T(8,128)(2,1)S(1)} %copy-done), kind=kOutput, calls=%fused_computation | convolution fusion | flops 1210318848 | bytes 7340032 | tf_op jit(solution)/shard_map/dot_general | solution.py:221
  122.9 74.5 %reduce-scatter.2.cloned.1.call-done = bf16[32,4608]{1,0:T(8,128)(2,1)} async-done(((bf16[512,4608]{1,0:T(8,128)(2,1)}), bf16[32,4608]{1,0:T(8,128)(2,1)}) %reduce-scatter.2.cloned.1.call-update) | async-done | bytes 294928 | tf_op jit(solution)/shard_map/reduce_scatter | solution.py:160
  198.5 1.3 fusion.25
  200.7 1.4 collective-permute-start.2
  202.1 3.7 %collective-permute-done.2 = bf16[32,2304]{1,0:T(8,128)(2,1)S(1)} collective-permute-done((bf16[32,2304]{1,0:T(8,128)(2,1)S(1)}, bf16[32,2304]{1,0:T(8,128)(2,1)S(1)}, u32[]{:S(2)}, u32[]{:S(2)}) %collective-permute-start.2) | collective-permute-done | bytes 147488 | tf_op jit(solution)/shard_map/ppermute | solution.py:152
  207.1 7.4 %convert.35 = bf16[2304,1280]{1,0:T(8,128)(2,1)} convert(f32[2304,1280]{1,0:T(8,128)} %param.21) | non-fusion elementwise | flops 2949120 | bytes 17694720 | tf_op jit(solution)/shard_map/convert.8
  214.5 7.5 %convert.34 = bf16[2304,1280]{1,0:T(8,128)(2,1)} convert(f32[2304,1280]{1,0:T(8,128)} %param.20) | non-fusion elementwise | flops 2949120 | bytes 17694720 | tf_op jit(solution)/shard_map/convert.9
  223.5 24.3 %all-gather.11.cloned.1.call-done = bf16[512,2304]{1,0:T(8,128)(2,1)} async-done(((bf16[32,2304]{1,0:T(8,128)(2,1)}), bf16[512,2304]{1,0:T(8,128)(2,1)}) %all-gather.11.cloned.1.call-update) | async-done | bytes 2359312 | tf_op jit(solution)/shard_map/all_gather | solution.py:156
  247.9 2.9 convolution_convert_fusion.2
  250.8 1.5 collective-permute-start.12
  252.4 2.8 convolution_convert_fusion.4
  255.8 1.5 convolution_convert_fusion.6
  257.4 1.4 collective-permute-start.8
  258.8 1.5 convolution_convert_fusion.8
  261.8 1.5 collective-permute-start.4
  263.3 1.5 convolution_convert_fusion.11
  264.8 1.5 convolution_convert_fusion.9
  266.4 1.5 convolution_convert_fusion.7
  267.9 1.5 convolution_convert_fusion.5
  269.4 1.5 convolution_convert_fusion.3
  271.0 11.0 %collective-permute-done.4 = bf16[512,256]{0,1:T(8,128)(2,1)} collective-permute-done((bf16[512,256]{0,1:T(8,128)(2,1)S(1)}, bf16[512,256]{0,1:T(8,128)(2,1)}, u32[]{:S(2)}, u32[]{:S(2)}) %collective-permute-start.4) | collective-permute-done | bytes 262176 | tf_op jit(solution)/shard_map/ppermute | solution.py:152
  281.9 1.5 collective-permute-start.3
  283.4 8.0 %all-gather.9.cloned.1.call-done = bf16[512,2304]{1,0:T(8,128)(2,1)} async-done(((bf16[32,2304]{1,0:T(8,128)(2,1)}), bf16[512,2304]{1,0:T(8,128)(2,1)}) %all-gather.9.cloned.1.call-update) | async-done | bytes 2359312 | tf_op jit(solution)/shard_map/all_gather | solution.py:156
  291.4 3.0 convolution_add_fusion.9
  294.5 1.5 collective-permute-start.5
  296.0 3.8 %fusion.47 = bf16[512,1280]{0,1:T(8,128)(2,1)} fusion(f32[512,256]{0,1:T(8,128)S(1)} %convolution_add_fusion.9, bf16[512,2304]{1,0:T(8,128)(2,1)} %all-gather.9.cloned.1.call-done, bf16[2304,1280]{1,0:T(8,128)(2,1)} %convert.34, bf16[512,256]{0,1:T(8,128)(2,1)S(1)} %collective-permute-done.3), kind=kOutput, calls=%fused_computation.81 | convolution fusion | flops 605552640 | bytes 4587520 | tf_op jit(solution)/shard_map/dot_general | solution.py:246
  300.5 2.2 convolution_add_fusion.7
  303.4 1.7 collective-permute-start.9
  305.1 1.9 fusion.65
  307.4 1.8 convolution_add_fusion.5
  309.2 1.7 fusion.83
  311.7 3.0 collective-permute-done.9
  314.7 1.7 fusion.101
  317.2 2.6 collective-permute-done.11
  319.8 1.7 fusion.119
  321.5 2.4 copy.30
  (104 shorter events, 22.4 us)
Async XLA Ops:
  7.2 112.1 %copy-start = (bf16[256,4608]{1,0:T(8,128)(2,1)S(1)}, bf16[256,4608]{1,0:T(8,128)(2,1)}, u32[]{:S(2)}) copy-start(bf16[256,4608]{1,0:T(8,128)(2,1)} %param.17) | copy-start | bytes 7077892
  7.2 54.5 %all-gather.7.cloned.1.call-start = ((), (), s32[]{:S(2)}) async-start(), calls=%async_computation.2 | async-start | bytes 2506752 | tf_op jit(solution)/shard_map/all_gather | solution.py:156
  10.3 6.8 %collective-permute-start = (bf16[32,2304]{1,0:T(8,128)(2,1)S(1)}, bf16[32,2304]{1,0:T(8,128)(2,1)S(1)}, u32[]{:S(2)}, u32[]{:S(2)}) collective-permute-start(bf16[32,2304]{1,0:T(8,128)(2,1)S(1)} %get-tuple-element.24), channel_id=1, source_target_pairs={{0,16},{16,0},{1,17},{17,1},{2,18},{18,2},{3,19},{19,3},{4,20},{20... | collective-permute-start | bytes 442376 | tf_op jit(solution)/shard_map/ppermute | solution.py:152
  17.1 0.7 copy-start.10
  17.8 87.2 %all-gather.5.cloned.1.call-start = ((), (), s32[]{:S(2)}) async-start(), calls=%async_computation.1 | async-start | bytes 2506752 | tf_op jit(solution)/shard_map/all_gather | solution.py:156
  18.5 178.8 %reduce-scatter.2.cloned.1.call-start = ((), (), s32[]{:S(2)}) async-start(), calls=%async_computation.3 | async-start | bytes 5013504 | tf_op jit(solution)/shard_map/reduce_scatter | solution.py:160
  18.6 4.0 %copy-start.4 = (f32[2304,128]{1,0:T(8,128)S(1)}, f32[2304,128]{1,0:T(8,128)}, u32[]{:S(2)}) copy-start(f32[2304,128]{1,0:T(8,128)} %param.16) | copy-start | bytes 3538948
  65.9 39.2 %collective-permute-start.1 = (bf16[512,512]{0,1:T(8,128)(2,1)}, bf16[512,512]{0,1:T(8,128)(2,1)}, u32[]{:S(2)}, u32[]{:S(2)}) collective-permute-start(bf16[512,512]{0,1:T(8,128)(2,1)} %convolution_convert_fusion.1), channel_id=1, source_target_pairs={{0,16},{16,0},{1,17},{17,1},{2,18},{18,2},{3,19},{19,3},{4,20},{20... | collective-permute-start | bytes 1572872 | tf_op jit(solution)/shard_map/ppermute | solution.py:152
  108.6 2.1 copy-start.6
  112.0 2.3 copy-start.9
  113.1 3.5 %copy-start.7 = (bf16[512,128]{0,1:T(8,128)(2,1)}, bf16[512,128]{0,1:T(8,128)(2,1)S(1)}, u32[]{:S(2)}) copy-start(bf16[512,128]{0,1:T(8,128)(2,1)S(1)} %get-tuple-element.31) | copy-start | bytes 393220
  122.8 75.7 %copy-start.3 = (bf16[32,4608]{1,0:T(8,128)(2,1)S(1)}, bf16[32,4608]{1,0:T(8,128)(2,1)}, u32[]{:S(2)}) copy-start(bf16[32,4608]{1,0:T(8,128)(2,1)} %param.11) | copy-start | bytes 884740
  122.8 75.7 %copy-start.13 = (f32[4608]{0:T(1024)S(1)}, f32[4608]{0:T(1024)}, u32[]{:S(2)}) copy-start(f32[4608]{0:T(1024)} %param.18) | copy-start | bytes 55300
  122.8 77.0 %copy-start.12 = (f32[4608]{0:T(1024)S(1)}, f32[4608]{0:T(1024)}, u32[]{:S(2)}) copy-start(f32[4608]{0:T(1024)} %param.19) | copy-start | bytes 55300
  122.9 125.0 %all-gather.11.cloned.1.call-start = ((), (), s32[]{:S(2)}) async-start(), calls=%async_computation.5 | async-start | bytes 2506752 | tf_op jit(solution)/shard_map/all_gather | solution.py:156
  199.8 14.7 %copy-start.5 = (bf16[32,4608]{1,0:T(8,128)(2,1)}, bf16[32,4608]{1,0:T(8,128)(2,1)S(1)}, u32[]{:S(2)}) copy-start(bf16[32,4608]{1,0:T(8,128)(2,1)S(1)} %get-tuple-element.17) | copy-start | bytes 884740
  200.7 5.1 %collective-permute-start.2 = (bf16[32,2304]{1,0:T(8,128)(2,1)S(1)}, bf16[32,2304]{1,0:T(8,128)(2,1)S(1)}, u32[]{:S(2)}, u32[]{:S(2)}) collective-permute-start(bf16[32,2304]{1,0:T(8,128)(2,1)S(1)} %get-tuple-element.22), channel_id=1, source_target_pairs={{0,16},{16,0},{1,17},{17,1},{2,18},{18,2},{3,19},{19,3},{4,20},{20... | collective-permute-start | bytes 442376 | tf_op jit(solution)/shard_map/ppermute | solution.py:152
  205.8 0.7 copy-start.11
  206.5 84.9 %all-gather.9.cloned.1.call-start = ((), (), s32[]{:S(2)}) async-start(), calls=%async_computation.4 | async-start | bytes 2506752 | tf_op jit(solution)/shard_map/all_gather | solution.py:156
  214.5 7.5 %copy-start.8 = (bf16[512,128]{0,1:T(8,128)(2,1)S(1)}, bf16[512,128]{0,1:T(8,128)(2,1)}, u32[]{:S(2)}) copy-start(bf16[512,128]{0,1:T(8,128)(2,1)} %copy-done.7) | copy-start | bytes 393220
  247.9 8.0 %copy-start.2 = (bf16[2304,1280]{1,0:T(8,128)(2,1)S(1)}, bf16[2304,1280]{1,0:T(8,128)(2,1)}, u32[]{:S(2)}) copy-start(bf16[2304,1280]{1,0:T(8,128)(2,1)} %convert.35) | copy-start | bytes 17694724
  250.8 5.0 %copy-start.15 = (bf16[512,2304]{1,0:T(8,128)(2,1)S(1)}, bf16[512,2304]{1,0:T(8,128)(2,1)}, u32[]{:S(2)}) copy-start(bf16[512,2304]{1,0:T(8,128)(2,1)} %all-gather.11.cloned.1.call-done) | copy-start | bytes 7077892
  250.8 65.5 %collective-permute-start.12 = (bf16[512,256]{0,1:T(8,128)(2,1)S(1)}, bf16[512,256]{0,1:T(8,128)(2,1)S(1)}, u32[]{:S(2)}, u32[]{:S(2)}) collective-permute-start(bf16[512,256]{0,1:T(8,128)(2,1)S(1)} %convolution_convert_fusion.2), channel_id=1, source_target_pairs={{0,16},{16,0},{1,17},{17,1},{2,18},{18,2},{3,19},{19,3},{4,20},{20... | collective-permute-start | bytes 786440 | tf_op jit(solution)/shard_map/ppermute | solution.py:152
  255.2 55.7 %collective-permute-start.10 = (bf16[512,256]{0,1:T(8,128)(2,1)S(1)}, bf16[512,256]{0,1:T(8,128)(2,1)S(1)}, u32[]{:S(2)}, u32[]{:S(2)}) collective-permute-start(bf16[512,256]{0,1:T(8,128)(2,1)S(1)} %convolution_convert_fusion.4), channel_id=1, source_target_pairs={{0,16},{16,0},{1,17},{17,1},{2,18},{18,2},{3,19},{19,3},{4,20},{20... | collective-permute-start | bytes 786440 | tf_op jit(solution)/shard_map/ppermute | solution.py:152
  255.8 7.4 %slice-start = ((s8[5898240]{0:T(1024)(128)(4,1)}), s8[4194304]{0:T(1024)(128)(4,1)S(1)}, s32[]{:S(2)}) async-start(s8[5898240]{0:T(1024)(128)(4,1)} %bitcast.47), calls=%async_computation.6 | async-start | bytes 8388608
  257.4 5.9 %slice-start.1 = ((s8[5898240]{0:T(1024)(128)(4,1)}), s8[1703936]{0:T(1024)(128)(4,1)S(1)}, s32[]{:S(2)}) async-start(s8[5898240]{0:T(1024)(128)(4,1)} %bitcast.47), calls=%async_computation.7 | async-start | bytes 3407872
  257.4 49.7 %collective-permute-start.8 = (bf16[512,256]{0,1:T(8,128)(2,1)}, bf16[512,256]{0,1:T(8,128)(2,1)}, u32[]{:S(2)}, u32[]{:S(2)}) collective-permute-start(bf16[512,256]{0,1:T(8,128)(2,1)} %convolution_convert_fusion.6), channel_id=1, source_target_pairs={{0,16},{16,0},{1,17},{17,1},{2,18},{18,2},{3,19},{19,3},{4,20},{20... | collective-permute-start | bytes 786440 | tf_op jit(solution)/shard_map/ppermute | solution.py:152
  260.3 39.5 %collective-permute-start.6 = (bf16[512,256]{0,1:T(8,128)(2,1)}, bf16[512,256]{0,1:T(8,128)(2,1)}, u32[]{:S(2)}, u32[]{:S(2)}) collective-permute-start(bf16[512,256]{0,1:T(8,128)(2,1)} %convolution_convert_fusion.8), channel_id=1, source_target_pairs={{0,16},{16,0},{1,17},{17,1},{2,18},{18,2},{3,19},{19,3},{4,20},{20... | collective-permute-start | bytes 786440 | tf_op jit(solution)/shard_map/ppermute | solution.py:152
  261.8 20.2 %collective-permute-start.4 = (bf16[512,256]{0,1:T(8,128)(2,1)S(1)}, bf16[512,256]{0,1:T(8,128)(2,1)}, u32[]{:S(2)}, u32[]{:S(2)}) collective-permute-start(bf16[512,256]{0,1:T(8,128)(2,1)S(1)} %convolution_convert_fusion.10), channel_id=1, source_target_pairs={{0,16},{16,0},{1,17},{17,1},{2,18},{18,2},{3,19},{19,3},{4,20},{20... | collective-permute-start | bytes 786440 | tf_op jit(solution)/shard_map/ppermute | solution.py:152
  271.0 23.5 %copy-start.19 = (bf16[512,256]{0,1:T(8,128)(2,1)S(1)}, bf16[512,256]{0,1:T(8,128)(2,1)}, u32[]{:S(2)}) copy-start(bf16[512,256]{0,1:T(8,128)(2,1)} %convolution_convert_fusion.9) | copy-start | bytes 786436
  281.9 12.5 %collective-permute-start.3 = (bf16[512,256]{0,1:T(8,128)(2,1)}, bf16[512,256]{0,1:T(8,128)(2,1)S(1)}, u32[]{:S(2)}, u32[]{:S(2)}) collective-permute-start(bf16[512,256]{0,1:T(8,128)(2,1)} %convolution_convert_fusion.11), channel_id=1, source_target_pairs={{0,16},{16,0},{1,17},{17,1},{2,18},{18,2},{3,19},{19,3},{4,20},{20... | collective-permute-start | bytes 786440 | tf_op jit(solution)/shard_map/ppermute | solution.py:152
  291.4 13.7 %slice-start.2 = ((s8[5898240]{0:T(1024)(128)(4,1)}), s8[4194304]{0:T(1024)(128)(4,1)S(1)}, s32[]{:S(2)}) async-start(s8[5898240]{0:T(1024)(128)(4,1)} %bitcast.49), calls=%async_computation.8 | async-start | bytes 8388608
  294.4 5.4 %copy-start.18 = (bf16[512,256]{0,1:T(8,128)(2,1)S(1)}, bf16[512,256]{0,1:T(8,128)(2,1)}, u32[]{:S(2)}) copy-start(bf16[512,256]{0,1:T(8,128)(2,1)} %convolution_convert_fusion.7) | copy-start | bytes 786436
  294.4 6.1 %copy-start.14 = (bf16[512,2304]{1,0:T(8,128)(2,1)S(1)}, bf16[512,2304]{1,0:T(8,128)(2,1)}, u32[]{:S(2)}) copy-start(bf16[512,2304]{1,0:T(8,128)(2,1)} %all-gather.9.cloned.1.call-done) | copy-start | bytes 7077892
  294.4 10.7 %slice-start.3 = ((s8[5898240]{0:T(1024)(128)(4,1)}), s8[1703936]{0:T(1024)(128)(4,1)S(1)}, s32[]{:S(2)}) async-start(s8[5898240]{0:T(1024)(128)(4,1)} %bitcast.49), calls=%async_computation.9 | async-start | bytes 3407872
  294.5 9.0 %collective-permute-start.5 = (bf16[512,256]{0,1:T(8,128)(2,1)S(1)}, bf16[512,256]{0,1:T(8,128)(2,1)S(1)}, u32[]{:S(2)}, u32[]{:S(2)}) collective-permute-start(bf16[512,256]{0,1:T(8,128)(2,1)S(1)} %copy-done.19), channel_id=1, source_target_pairs={{0,16},{16,0},{1,17},{17,1},{2,18},{18,2},{3,19},{19,3},{4,20},{20... | collective-permute-start | bytes 786440 | tf_op jit(solution)/shard_map/ppermute | solution.py:152
  296.0 11.4 %slice-start.4 = ((s8[5898240]{0:T(1024)(128)(4,1)}), s8[4194304]{0:T(1024)(128)(4,1)S(1)}, s32[]{:S(2)}) async-start(s8[5898240]{0:T(1024)(128)(4,1)} %bitcast.51), calls=%async_computation.10 | async-start | bytes 8388608
  299.8 3.6 %copy-start.17 = (bf16[512,256]{0,1:T(8,128)(2,1)S(1)}, bf16[512,256]{0,1:T(8,128)(2,1)}, u32[]{:S(2)}) copy-start(bf16[512,256]{0,1:T(8,128)(2,1)} %convolution_convert_fusion.5) | copy-start | bytes 786436
  299.8 7.6 %slice-start.5 = ((s8[5898240]{0:T(1024)(128)(4,1)}), s8[1703936]{0:T(1024)(128)(4,1)S(1)}, s32[]{:S(2)}) async-start(s8[5898240]{0:T(1024)(128)(4,1)} %bitcast.51), calls=%async_computation.11 | async-start | bytes 3407872
  299.8 9.4 %collective-permute-start.7 = (bf16[512,256]{0,1:T(8,128)(2,1)S(1)}, bf16[512,256]{0,1:T(8,128)(2,1)S(1)}, u32[]{:S(2)}, u32[]{:S(2)}) collective-permute-start(bf16[512,256]{0,1:T(8,128)(2,1)S(1)} %copy-done.18), channel_id=1, source_target_pairs={{0,16},{16,0},{1,17},{17,1},{2,18},{18,2},{3,19},{19,3},{4,20},{20... | collective-permute-start | bytes 786440 | tf_op jit(solution)/shard_map/ppermute | solution.py:152
  302.7 4.4 %copy-start.16 = (bf16[512,256]{0,1:T(8,128)(2,1)S(1)}, bf16[512,256]{0,1:T(8,128)(2,1)}, u32[]{:S(2)}) copy-start(bf16[512,256]{0,1:T(8,128)(2,1)} %convolution_convert_fusion.3) | copy-start | bytes 786436
  303.4 11.3 %collective-permute-start.9 = (bf16[512,256]{0,1:T(8,128)(2,1)S(1)}, bf16[512,256]{0,1:T(8,128)(2,1)S(1)}, u32[]{:S(2)}, u32[]{:S(2)}) collective-permute-start(bf16[512,256]{0,1:T(8,128)(2,1)S(1)} %copy-done.17), channel_id=1, source_target_pairs={{0,16},{16,0},{1,17},{17,1},{2,18},{18,2},{3,19},{19,3},{4,20},{20... | collective-permute-start | bytes 786440 | tf_op jit(solution)/shard_map/ppermute | solution.py:152
  307.1 12.8 %collective-permute-start.11 = (bf16[512,256]{0,1:T(8,128)(2,1)S(1)}, bf16[512,256]{0,1:T(8,128)(2,1)S(1)}, u32[]{:S(2)}, u32[]{:S(2)}) collective-permute-start(bf16[512,256]{0,1:T(8,128)(2,1)S(1)} %copy-done.16), channel_id=1, source_target_pairs={{0,16},{16,0},{1,17},{17,1},{2,18},{18,2},{3,19},{19,3},{4,20},{20... | collective-permute-start | bytes 786440 | tf_op jit(solution)/shard_map/ppermute | solution.py:152
  319.8 4.1 %copy-start.1 = (bf16[256,4608]{1,0:T(8,128)(2,1)S(1)}, bf16[256,4608]{1,0:T(8,128)(2,1)}, u32[]{:S(2)}) copy-start(bf16[256,4608]{1,0:T(8,128)(2,1)} %param.17) | copy-start | bytes 7077892
Sparse Core Ops, SparseCore 0:
  17.9 43.7 all-gather.6
  63.9 41.0 all-gather.4
  123.0 74.3 reduce-scatter.1
  206.6 41.1 all-gather.10
  250.3 41.0 all-gather.8

commit v2 on v1

--- a/solution.py
+++ b/solution.py
@@ -1,8 +1,11 @@
+import functools
 import math
 
 import jax
 import jax.numpy as jnp
 from jax import lax
+from jax.experimental import pallas as pl
+from jax.experimental.pallas import tpu as pltpu
 from jax.sharding import PartitionSpec as P
 
 KVH = 16
@@ -152,12 +155,230 @@
     return lax.ppermute(value, "dp", [(0, 1), (1, 0)])
 
 
-def gather_mp(block):
-    return lax.all_gather(block, "mp", axis=0, tiled=True)
-
-
-def scatter_mp(partial):
-    return lax.psum_scatter(partial, "mp", scatter_dimension=0, tiled=True)
+def place_of():
+    me = lax.axis_index("mp")
+    return me, me // 4, (me // 2) % 2, me % 2
+
+
+def index_of(z, y, core):
+    return z * 4 + y * 2 + core
+
+
+def greet(peers):
+    barrier = pltpu.get_barrier_semaphore()
+    for peer in peers:
+        pl.semaphore_signal(barrier, inc=1, device_id=peer, device_id_type=pl.DeviceIdType.MESH)
+    pl.semaphore_wait(barrier, len(peers))
+
+
+def mp_peers():
+    me, z, y, core = place_of()
+    along_z = [{"mp": index_of(lax.rem(z + step, 4), y, core)} for step in (1, 2, 3)]
+    return along_z, {"mp": index_of(z, 1 - y, core)}, {"mp": index_of(z, y, 1 - core)}
+
+
+def gather_kernel(from_partner, block_ref, out_ref, send_sem, recv_sem):
+    me, z, y, core = place_of()
+    along_z, across_y, sibling = mp_peers()
+    partner = {"dp": 1 - lax.axis_index("dp")}
+    greet(along_z + [across_y, sibling] + ([partner] if from_partner else []))
+    started = []
+
+    def copy(source, slot, peer):
+        return pltpu.make_async_remote_copy(
+            src_ref=source,
+            dst_ref=out_ref.at[slot],
+            send_sem=send_sem.at[len(started)],
+            recv_sem=recv_sem.at[slot],
+            device_id=peer,
+            device_id_type=pl.DeviceIdType.MESH,
+        )
+
+    def send(source, slot, peer):
+        one = copy(source, slot, peer)
+        one.start()
+        started.append(one)
+
+    def arrive(slot, peer):
+        pltpu.make_async_remote_copy(
+            src_ref=out_ref.at[slot],
+            dst_ref=out_ref.at[slot],
+            send_sem=send_sem.at[0],
+            recv_sem=recv_sem.at[slot],
+            device_id=peer,
+            device_id_type=pl.DeviceIdType.MESH,
+        ).wait_recv()
+
+    if from_partner:
+        send(block_ref, me, partner)
+        arrive(me, partner)
+    else:
+        out_ref[me] = block_ref[...]
+    mine = out_ref.at[me]
+    for peer in along_z:
+        send(mine, me, peer)
+    send(mine, me, across_y)
+    send(mine, me, sibling)
+    for step in (1, 2, 3):
+        slot = index_of(lax.rem(z + step, 4), y, core)
+        arrive(slot, along_z[step - 1])
+        send(out_ref.at[slot], slot, across_y)
+        send(out_ref.at[slot], slot, sibling)
+    for step in range(4):
+        slot = index_of(lax.rem(z + step, 4), 1 - y, core)
+        arrive(slot, across_y)
+        send(out_ref.at[slot], slot, sibling)
+    for step in range(4):
+        for row in (y, 1 - y):
+            arrive(index_of(lax.rem(z + step, 4), row, 1 - core), sibling)
+    for one in started:
+        one.wait_send()
+
+
+def gather_mp(block, from_partner, collective_id):
+    count = lax.axis_size("mp")
+    rows, columns = block.shape
+    out = pl.pallas_call(
+        functools.partial(gather_kernel, from_partner),
+        out_shape=jax.ShapeDtypeStruct((count, rows, columns), block.dtype),
+        in_specs=[pl.BlockSpec(memory_space=pltpu.VMEM)],
+        out_specs=pl.BlockSpec(memory_space=pltpu.VMEM),
+        scratch_shapes=[
+            pltpu.SemaphoreType.DMA((count,)),
+            pltpu.SemaphoreType.DMA((count,)),
+        ],
+        compiler_params=pltpu.CompilerParams(
+            collective_id=collective_id, has_side_effects=True, vmem_limit_bytes=32 * 2**20
+        ),
+        cost_estimate=pl.CostEstimate(flops=15 * 10**9, bytes_accessed=10**7, transcendentals=0),
+    )(block)
+    return out.reshape(count * rows, columns)
+
+
+def scatter_kernel(
+    part_ref, out_ref, core_buf, y_buf, z_buf, core_send, core_recv, y_send, y_recv, z_send, z_recv
+):
+    me, z, y, core = place_of()
+    along_z, across_y, sibling = mp_peers()
+    greet(along_z + [across_y, sibling])
+    rows, columns = out_ref.shape
+    width = columns // 9
+    started = []
+
+    def copy(source, target, send_sem, recv_sem, peer):
+        return pltpu.make_async_remote_copy(
+            src_ref=source,
+            dst_ref=target,
+            send_sem=send_sem,
+            recv_sem=recv_sem,
+            device_id=peer,
+            device_id_type=pl.DeviceIdType.MESH,
+        )
+
+    def core_copy(zz, yy, target_core):
+        place = zz * 2 + yy
+        return copy(
+            part_ref.at[index_of(zz, yy, target_core)],
+            core_buf.at[place],
+            core_send.at[place],
+            core_recv.at[place],
+            sibling,
+        )
+
+    order = [lax.rem(z + step, 4) for step in (2, 1, 3, 0)]
+    for yy in (1 - y, y):
+        for zz in order:
+            one = core_copy(zz, yy, 1 - core)
+            one.start()
+            started.append(one)
+
+    def add_core(zz, yy):
+        core_copy(zz, yy, core).wait_recv()
+        place, slot = zz * 2 + yy, index_of(zz, yy, core)
+        for start in range(0, columns, width):
+            cut = pl.ds(start, width)
+            total = core_buf[place, :, cut].astype(jnp.float32) + part_ref[slot, :, cut].astype(
+                jnp.float32
+            )
+            core_buf[place, :, cut] = total.astype(core_buf.dtype)
+
+    def y_copy(zz, yy):
+        return copy(
+            core_buf.at[zz * 2 + yy], y_buf.at[zz], y_send.at[zz], y_recv.at[zz], across_y
+        )
+
+    for zz in order:
+        add_core(zz, 1 - y)
+        one = y_copy(zz, 1 - y)
+        one.start()
+        started.append(one)
+
+    def z_copy(zz, source_z, peer):
+        return copy(
+            core_buf.at[zz * 2 + y],
+            z_buf.at[source_z],
+            z_send.at[zz],
+            z_recv.at[source_z],
+            peer,
+        )
+
+    for step in (2, 1, 3, 0):
+        zz = lax.rem(z + step, 4)
+        add_core(zz, y)
+        y_copy(zz, y).wait_recv()
+        if step == 0:
+            continue
+        place = zz * 2 + y
+        for start in range(0, columns, width):
+            cut = pl.ds(start, width)
+            total = core_buf[place, :, cut].astype(jnp.float32) + y_buf[zz, :, cut].astype(
+                jnp.float32
+            )
+            core_buf[place, :, cut] = total.astype(core_buf.dtype)
+        one = z_copy(zz, z, along_z[step - 1])
+        one.start()
+        started.append(one)
+    for step in (1, 3, 2):
+        zz = lax.rem(z + step, 4)
+        z_copy(zz, zz, along_z[step - 1]).wait_recv()
+    for start in range(0, columns, width):
+        cut = pl.ds(start, width)
+        total = core_buf[z * 2 + y, :, cut].astype(jnp.float32) + y_buf[z, :, cut].astype(
+            jnp.float32
+        )
+        for step in (1, 2, 3):
+            total = total + z_buf[lax.rem(z + step, 4), :, cut].astype(jnp.float32)
+        out_ref[:, cut] = total
+    for one in started:
+        one.wait_send()
+
+
+def scatter_mp(partial, collective_id):
+    count = lax.axis_size("mp")
+    tokens, columns = partial.shape
+    rows = tokens // count
+    dma = pltpu.SemaphoreType.DMA
+    return pl.pallas_call(
+        scatter_kernel,
+        out_shape=jax.ShapeDtypeStruct((rows, columns), jnp.float32),
+        in_specs=[pl.BlockSpec(memory_space=pltpu.VMEM)],
+        out_specs=pl.BlockSpec(memory_space=pltpu.VMEM),
+        scratch_shapes=[
+            pltpu.VMEM((8, rows, columns), partial.dtype),
+            pltpu.VMEM((4, rows, columns), partial.dtype),
+            pltpu.VMEM((4, rows, columns), partial.dtype),
+            dma((8,)),
+            dma((8,)),
+            dma((4,)),
+            dma((4,)),
+            dma((4,)),
+            dma((4,)),
+        ],
+        compiler_params=pltpu.CompilerParams(
+            collective_id=collective_id, has_side_effects=True, vmem_limit_bytes=40 * 2**20
+        ),
+        cost_estimate=pl.CostEstimate(flops=30 * 10**9, bytes_accessed=10**7, transcendentals=0),
+    )(partial.reshape(count, rows, columns))
 
 
 def split_rows(block):
@@ -166,15 +387,6 @@
     own = lax.dynamic_slice_in_dim(block, index * half, half, 1)
     other = lax.dynamic_slice_in_dim(block, (1 - index) * half, half, 1)
     return own, other
-
-
-def exchange_gather(block):
-    own, other = split_rows(block)
-    arrived = swap_dp(other)
-    own, arrived = lax.optimization_barrier((own, arrived))
-    partner_tokens = gather_mp(arrived)
-    own_tokens = gather_mp(own)
-    return own_tokens, partner_tokens
 
 
 def on_device_pair(
@@ -194,12 +406,16 @@
     slot = inputs.shape[0] * lax.axis_size("mp")
     length = lengths[0]
     normed_local = rms_norm(inputs.astype(jnp.float32), gain_in).astype(bf16)
-    own_tokens, partner_tokens = exchange_gather(normed_local)
+    own_rows, other_rows = split_rows(normed_local)
+    partner_tokens = gather_mp(other_rows, True, 0)
     qkv_weight = jnp.concatenate([query_weight, key_weight, value_weight], axis=1).astype(bf16)
     head_size = key_weight.shape[1]
     local_heads = query_weight.shape[1] // head_size
     partner_part = jnp.dot(partner_tokens, qkv_weight, preferred_element_type=jnp.float32)
-    arrived = swap_dp(partner_part.astype(bf16))
+    partner_part = partner_part.astype(bf16)
+    own_rows = lax.optimization_barrier((partner_part, own_rows))[1]
+    arrived = swap_dp(partner_part)
+    own_tokens = gather_mp(own_rows, False, 1)
     raw = jnp.dot(own_tokens, qkv_weight, preferred_element_type=jnp.float32)
     raw = raw + arrived.astype(jnp.float32)
     q_cols = local_heads * head_size
@@ -218,28 +434,30 @@
     mixed = jnp.where(live[:, None, None], mixed, jnp.float32(0.0))
     attended = mixed.astype(bf16).reshape(slot, local_heads * head_size)
     attn_rows = scatter_mp(
-        jnp.dot(attended, output_weight, preferred_element_type=jnp.float32).astype(bf16)
-    ).astype(jnp.float32)
+        jnp.dot(attended, output_weight, preferred_element_type=jnp.float32).astype(bf16), 2
+    )
     residual = (inputs.astype(jnp.float32) + rms_norm(attn_rows, gain_post)).astype(bf16)
     pre_local = rms_norm(residual.astype(jnp.float32), gain_pre).astype(bf16)
-    own_tokens, partner_tokens = exchange_gather(pre_local)
+    own_rows, other_rows = split_rows(pre_local)
+    partner_tokens = gather_mp(other_rows, True, 3)
     columns = gate_weight.shape[1]
     width = 256
     weights = []
-    sent = []
+    parts = []
     for start in range(0, columns, width):
         pair = tuple(
             weight[:, start : start + width].astype(bf16) for weight in (gate_weight, up_weight)
         )
         weights.append(pair)
-        sent.append(
+        parts.append(
             tuple(
-                swap_dp(
-                    jnp.dot(partner_tokens, piece, preferred_element_type=jnp.float32).astype(bf16)
-                )
+                jnp.dot(partner_tokens, piece, preferred_element_type=jnp.float32).astype(bf16)
                 for piece in pair
             )
         )
+    own_rows = lax.optimization_barrier((parts, own_rows))[1]
+    sent = [tuple(swap_dp(part) for part in pair) for pair in parts]
+    own_tokens = gather_mp(own_rows, False, 4)
     hidden = []
     for pair, arrived in zip(weights, sent):
         gate, up_part = tuple(
@@ -252,7 +470,7 @@
 
 
 def solution(mesh):
-    pair_form = mesh.shape["dp"] == 2 and mesh.shape["mp"] <= KVH
+    pair_form = mesh.shape["dp"] == 2 and mesh.shape["mp"] == KVH
     in_specs = (
         P(("dp", "mp"), None),
         P("dp"),

time: 331 us -> 251 us (0.76)
  waiting for transfers between devices: 205 us -> 21.8 us
  Pallas kernels: 0 us -> 156 us
  matrix products: 52.9 us -> 25.2 us
  between operations: 14.8 us -> 1.84 us
  starting transfers between devices: 17.7 us -> 11.4 us
  local copies, waits for them, and re-layouts: 8.9 us -> 4.79 us
    pallas_call x0 -> x5, Pallas kernels: none -> 156 us  [the longest x4 113 us: gather_mp(): pl.pallas_call(functools.partial(gather_kernel, from_partner), out_shape=...]
    all_gather x4 -> x0, waiting for transfers between devices: 105 us -> none  [gather_mp(): return lax.all_gather(block, 'mp', axis=0, tiled=True)]
    reduce_scatter x1 -> x0, waiting for transfers between devices: 74.5 us -> none  [scatter_mp(): return lax.psum_scatter(partial, 'mp', scatter_dimension=0, tiled=True)]
    dot_general x10, matrix products: 19.3 us -> 8.32 us  [on_device_pair(): jnp.dot(own_tokens, piece, preferred_element_type=jnp.float32)]
    dot_general x10, matrix products: 17.3 us -> 7.77 us  [on_device_pair(): jnp.dot(partner_tokens, piece, preferred_element_type=jnp.float32)]
    ppermute x13 -> x11, starting transfers between devices: 17.3 us -> 11.4 us  [swap_dp(): return lax.ppermute(value, 'dp', [(0, 1), (1, 0)])]
    unnamed x57 -> x44, local copies, waits for them, and re-layouts: 6.71 us -> 1.87 us
    ppermute x13 -> x11, waiting for transfers between devices: 24.9 us -> 21.8 us  [swap_dp(): return lax.ppermute(value, 'dp', [(0, 1), (1, 0)])]
  transfers between devices with their start and end apart: 18 -> 11, of which waited for: 11 -> 4; matrix products, arithmetic and copies ran while one was open for 19% -> 10% of each run, Pallas kernels for 0% -> 22%
where the time goes in v2:
time: 251 us; the launch traced here: 250 us
  Pallas kernels  156 us (62%)
  other arithmetic  28.4 us (11%)
  matrix products  25.2 us (10%)
  waiting for transfers between devices  21.8 us (9%)
  starting transfers between devices  11.4 us (5%)
  local copies, waits for them, and re-layouts  4.79 us (2%)
    pallas_call x4, Pallas kernels, gather_mp(): pl.pallas_call(functools.partial(gather_kernel, from_partner), out_shape=...  113 us
    pallas_call x1, Pallas kernels, scatter_mp(): pl.pallas_call(scatter_kernel, out_shape=jax.ShapeDtypeStruct((rows, colu...  42.9 us
    ppermute x11, waiting for transfers between devices, swap_dp(): return lax.ppermute(value, 'dp', [(0, 1), (1, 0)])  21.8 us
    another operation x6, other arithmetic  20 us
    ppermute x11, starting transfers between devices, swap_dp(): return lax.ppermute(value, 'dp', [(0, 1), (1, 0)])  11.4 us
    dot_general x10, matrix products, on_device_pair(): jnp.dot(own_tokens, piece, preferred_element_type=jnp.float32)  8.32 us
    dot_general x10, matrix products, on_device_pair(): jnp.dot(partner_tokens, piece, preferred_element_type=jnp.float32)  7.77 us
  transfers between devices with their start and end apart: 11, of which 4 were waited for; matrix products, arithmetic and copies ran while one was open for 10% of the time, Pallas kernels for 22%

profile of v2, /device:TPU:0, one launch (start us, length us, event | category | flops | bytes accessed | tf_op | source)
XLA Modules:
  0.0 249.8 jit_solution(11308912858975395040)
XLA Ops:
  0.7 1.3 fusion.37
  2.0 1.4 convert.30
  3.4 2.4 convert.31
  5.8 1.1 convert.29
  7.1 32.0 %shard_map.138 = bf16[16,32,2304]{2,1,0:T(8,128)(2,1)S(1)} custom-call(bf16[32,2304]{1,0:T(8,128)(2,1)S(1)} %get-tuple-element.17.block_ref), custom_call_target="tpu_custom_call" | custom-call | flops 15000000512 | bytes 10000000 | tf_op jit(solution)/shard_map/pallas_call | solution.py:241
  39.1 1.4 convolution_convert_fusion.1
  40.5 0.9 collective-permute-start
  42.1 26.0 %shard_map.139 = bf16[16,32,2304]{2,1,0:T(8,128)(2,1)S(1)} custom-call(bf16[32,2304]{1,0:T(8,128)(2,1)S(1)} %get-tuple-element.6.block_ref), custom_call_target="tpu_custom_call" | custom-call | flops 15000000512 | bytes 10000000 | tf_op jit(solution)/shard_map/pallas_call | solution.py:241
  68.1 7.4 %convert.34 = bf16[2304,1280]{1,0:T(8,128)(2,1)} convert(f32[2304,1280]{1,0:T(8,128)} %param.20) | non-fusion elementwise | flops 2949120 | bytes 17694720 | tf_op jit(solution)/shard_map/convert.9
  75.6 7.5 %convert.35 = bf16[2304,1280]{1,0:T(8,128)(2,1)} convert(f32[2304,1280]{1,0:T(8,128)} %param.21) | non-fusion elementwise | flops 2949120 | bytes 17694720 | tf_op jit(solution)/shard_map/convert.8
  83.1 0.8 fusion.2
  83.9 1.7 multiply_cosine_fusion
  85.7 1.4 convert_add_fusion
  87.1 0.9 slice.82
  88.2 1.8 fusion.90
  90.1 1.3 reshape.209
  92.0 1.9 fusion.97
  94.0 2.2 bitcast_select_fusion
  96.3 2.7 %fusion = bf16[128,2,512]{2,0,1:T(8,128)(2,1)S(1)} fusion(f32[2,512,512]{1,2,0:T(8,128)} %bitcast_select_fusion, pred[512]{0:T(512)(128)(4,1)S(1)} %iota_compare_fusion.1, bf16[512,128]{1,0:T(8,128)(2,1)S(1)} %copy-done.12), kind=kOutput, calls=%fused_computation.6 | convolution fusion | flops 135529984 | bytes 2490880 | tf_op jit(solution)/shard_map/hqk,kd->qhd/dot_general | solution.py:61
  99.0 1.4 convolution_convert_fusion
  100.4 42.9 %shard_map.140 = f32[32,4608]{1,0:T(8,128)S(1)} custom-call(bf16[16,32,4608]{2,1,0:T(8,128)(2,1)S(1)} %bitcast.51), custom_call_target="tpu_custom_call" | custom-call | flops 30000001024 | bytes 10000000 | tf_op jit(solution)/shard_map/pallas_call | solution.py:361
  144.1 26.2 %shard_map.141 = bf16[16,32,2304]{2,1,0:T(8,128)(2,1)S(1)} custom-call(bf16[32,2304]{1,0:T(8,128)(2,1)S(1)} %get-tuple-element.15.block_ref), custom_call_target="tpu_custom_call" | custom-call | flops 15000000512 | bytes 10000000 | tf_op jit(solution)/shard_map/pallas_call | solution.py:241
  170.3 0.8 convolution_convert_fusion.3
  171.1 0.8 convolution_convert_fusion.5
  171.9 0.8 convolution_convert_fusion.7
  172.7 0.8 convolution_convert_fusion.9
  173.4 0.8 convolution_convert_fusion.11
  175.6 0.8 convolution_convert_fusion.4
  176.3 0.8 convolution_convert_fusion.6
  177.1 0.8 convolution_convert_fusion.8
  177.9 0.8 convolution_convert_fusion.10
  179.3 1.5 collective-permute-start.3
  181.3 1.5 collective-permute-start.7
  183.3 29.3 %shard_map.142 = bf16[16,32,2304]{2,1,0:T(8,128)(2,1)S(1)} custom-call(bf16[32,2304]{1,0:T(8,128)(2,1)S(1)} %get-tuple-element.7.block_ref), custom_call_target="tpu_custom_call" | custom-call | flops 15000000512 | bytes 10000000 | tf_op jit(solution)/shard_map/pallas_call | solution.py:241
  212.6 1.0 fusion.6
  216.8 1.7 collective-permute-start.9
  218.9 0.8 fusion.96
  219.8 1.7 collective-permute-start.6
  221.5 10.2 %collective-permute-done.4 = bf16[512,256]{1,0:T(8,128)(2,1)S(1)} collective-permute-done((bf16[512,256]{1,0:T(8,128)(2,1)S(1)}, bf16[512,256]{1,0:T(8,128)(2,1)S(1)}, u32[]{:S(2)}, u32[]{:S(2)}) %collective-permute-start.4) | collective-permute-done | bytes 262176 | tf_op jit(solution)/shard_map/ppermute | solution.py:155
  231.6 1.6 collective-permute-start.8
  233.2 0.8 fusion.95
  234.6 2.7 %collective-permute-done.6 = bf16[512,256]{1,0:T(8,128)(2,1)S(1)} collective-permute-done((bf16[512,256]{1,0:T(8,128)(2,1)S(1)}, bf16[512,256]{1,0:T(8,128)(2,1)S(1)}, u32[]{:S(2)}, u32[]{:S(2)}) %collective-permute-start.6) | collective-permute-done | bytes 262176 | tf_op jit(solution)/shard_map/ppermute | solution.py:155
  237.2 0.8 fusion.94
  238.1 4.8 %collective-permute-done.8 = bf16[512,256]{1,0:T(8,128)(2,1)S(1)} collective-permute-done((bf16[512,256]{1,0:T(8,128)(2,1)S(1)}, bf16[512,256]{1,0:T(8,128)(2,1)S(1)}, u32[]{:S(2)}, u32[]{:S(2)}) %collective-permute-start.8) | collective-permute-done | bytes 262176 | tf_op jit(solution)/shard_map/ppermute | solution.py:155
  242.9 0.8 fusion.93
  243.7 4.2 %collective-permute-done.10 = bf16[512,256]{1,0:T(8,128)(2,1)S(1)} collective-permute-done((bf16[512,256]{1,0:T(8,128)(2,1)S(1)}, bf16[512,256]{1,0:T(8,128)(2,1)S(1)}, u32[]{:S(2)}, u32[]{:S(2)}) %collective-permute-start.10) | collective-permute-done | bytes 262176 | tf_op jit(solution)/shard_map/ppermute | solution.py:155
  247.9 0.8 fusion.92
  248.8 1.0 copy-done.17
  (77 shorter events, 8.9 us)
Async XLA Ops:
  0.6 98.4 %copy-start = (bf16[256,4608]{1,0:T(8,128)(2,1)S(1)}, bf16[256,4608]{1,0:T(8,128)(2,1)}, u32[]{:S(2)}) copy-start(bf16[256,4608]{1,0:T(8,128)(2,1)} %param.17) | copy-start | bytes 7077892
  0.7 5.1 %copy-start.3 = (f32[2304,256]{1,0:T(8,128)S(1)}, f32[2304,256]{1,0:T(8,128)}, u32[]{:S(2)}) copy-start(f32[2304,256]{1,0:T(8,128)} %param.14) | copy-start | bytes 7077892
  3.4 35.7 %copy-start.8 = (bf16[2304,128]{1,0:T(8,128)(2,1)}, bf16[2304,128]{1,0:T(8,128)(2,1)S(1)}, u32[]{:S(2)}) copy-start(bf16[2304,128]{1,0:T(8,128)(2,1)S(1)} %convert.30) | copy-start | bytes 1769476
  3.4 3.5 %copy-start.2 = (bf16[32,4608]{1,0:T(8,128)(2,1)S(1)}, bf16[32,4608]{1,0:T(8,128)(2,1)}, u32[]{:S(2)}) copy-start(bf16[32,4608]{1,0:T(8,128)(2,1)} %param.11) | copy-start | bytes 884740
  3.4 3.5 %copy-start.14 = (f32[4608]{0:T(1024)S(1)}, f32[4608]{0:T(1024)}, u32[]{:S(2)}) copy-start(f32[4608]{0:T(1024)} %param.13) | copy-start | bytes 55300
  7.1 32.0 %copy-start.4 = (bf16[2304,256]{1,0:T(8,128)(2,1)S(1)}, bf16[2304,256]{1,0:T(8,128)(2,1)}, u32[]{:S(2)}) copy-start(bf16[2304,256]{1,0:T(8,128)(2,1)} %convert.29) | copy-start | bytes 3538948
  7.1 32.0 %copy-start.10 = (bf16[2304,128]{1,0:T(8,128)(2,1)S(1)}, bf16[2304,128]{1,0:T(8,128)(2,1)}, u32[]{:S(2)}) copy-start(bf16[2304,128]{1,0:T(8,128)(2,1)} %convert.31) | copy-start | bytes 1769476
  40.5 45.2 %collective-permute-start = (bf16[512,512]{1,0:T(8,128)(2,1)S(1)}, bf16[512,512]{1,0:T(8,128)(2,1)S(1)}, u32[]{:S(2)}, u32[]{:S(2)}) collective-permute-start(bf16[512,512]{1,0:T(8,128)(2,1)S(1)} %convolution_convert_fusion.1), channel_id=1, source_target_pairs={{0,16},{16,0},{1,17},{17,1},{2,18},{18,2},{3,19},{19,3},{4,20},{20... | collective-permute-start | bytes 1572872 | tf_op jit(solution)/shard_map/ppermute | solution.py:155
  75.6 10.1 %copy-start.9 = (bf16[2304,128]{1,0:T(8,128)(2,1)S(1)}, bf16[2304,128]{1,0:T(8,128)(2,1)}, u32[]{:S(2)}) copy-start(bf16[2304,128]{1,0:T(8,128)(2,1)} %copy-done.8) | copy-start | bytes 1769476
  87.1 1.1 copy-start.7
  91.4 2.5 %copy-start.6 = (f32[512,64]{1,0:T(8,128)S(1)}, f32[512,64]{1,0:T(8,128)}, u32[]{:S(2)}) copy-start(f32[512,64]{1,0:T(8,128)} %get-tuple-element.21) | copy-start | bytes 393220
  91.4 2.7 %copy-start.11 = (pred[512,512]{0,1:T(8,128)(4,1)S(1)}, pred[512,512]{0,1:T(8,128)(4,1)}, u32[]{:S(2)}) copy-start(pred[512,512]{0,1:T(8,128)(4,1)} %fusion.2) | copy-start | bytes 786436
  93.9 2.4 copy-start.13
  94.0 2.3 copy-start.12
  100.4 43.1 %copy-start.16 = (f32[4608]{0:T(1024)S(1)}, f32[4608]{0:T(1024)}, u32[]{:S(2)}) copy-start(f32[4608]{0:T(1024)} %param.18) | copy-start | bytes 55300
  100.4 43.4 %copy-start.15 = (f32[4608]{0:T(1024)S(1)}, f32[4608]{0:T(1024)}, u32[]{:S(2)}) copy-start(f32[4608]{0:T(1024)} %param.19) | copy-start | bytes 55300
  143.5 26.8 %slice-start.2 = ((s8[5898240]{0:T(1024)(128)(4,1)}), s8[4194304]{0:T(1024)(128)(4,1)S(1)}, s32[]{:S(2)}) async-start(s8[5898240]{0:T(1024)(128)(4,1)} %bitcast.76), calls=%async_computation.2 | async-start | bytes 8388608
  143.8 26.4 %copy-start.5 = (bf16[32,4608]{1,0:T(8,128)(2,1)}, bf16[32,4608]{1,0:T(8,128)(2,1)S(1)}, u32[]{:S(2)}) copy-start(bf16[32,4608]{1,0:T(8,128)(2,1)S(1)} %get-tuple-element.9) | copy-start | bytes 884740
  144.0 26.2 %slice-start.3 = ((s8[5898240]{0:T(1024)(128)(4,1)}), s8[1703936]{0:T(1024)(128)(4,1)S(1)}, s32[]{:S(2)}) async-start(s8[5898240]{0:T(1024)(128)(4,1)} %bitcast.76), calls=%async_computation.3 | async-start | bytes 3407872
  171.9 2.4 slice-start
  172.6 2.1 slice-start.1
  178.7 38.1 %collective-permute-start.1 = (bf16[512,256]{1,0:T(8,128)(2,1)S(1)}, bf16[512,256]{1,0:T(8,128)(2,1)S(1)}, u32[]{:S(2)}, u32[]{:S(2)}) collective-permute-start(bf16[512,256]{1,0:T(8,128)(2,1)S(1)} %convolution_convert_fusion.11), channel_id=1, source_target_pairs={{0,16},{16,0},{1,17},{17,1},{2,18},{18,2},{3,19},{19,3},{4,20},{20... | collective-permute-start | bytes 786440 | tf_op jit(solution)/shard_map/ppermute | solution.py:155
  179.3 40.5 %collective-permute-start.3 = (bf16[512,256]{1,0:T(8,128)(2,1)S(1)}, bf16[512,256]{1,0:T(8,128)(2,1)S(1)}, u32[]{:S(2)}, u32[]{:S(2)}) collective-permute-start(bf16[512,256]{1,0:T(8,128)(2,1)S(1)} %convolution_convert_fusion.9), channel_id=1, source_target_pairs={{0,16},{16,0},{1,17},{17,1},{2,18},{18,2},{3,19},{19,3},{4,20},{20... | collective-permute-start | bytes 786440 | tf_op jit(solution)/shard_map/ppermute | solution.py:155
  180.8 53.3 %collective-permute-start.5 = (bf16[512,256]{1,0:T(8,128)(2,1)S(1)}, bf16[512,256]{1,0:T(8,128)(2,1)S(1)}, u32[]{:S(2)}, u32[]{:S(2)}) collective-permute-start(bf16[512,256]{1,0:T(8,128)(2,1)S(1)} %convolution_convert_fusion.7), channel_id=1, source_target_pairs={{0,16},{16,0},{1,17},{17,1},{2,18},{18,2},{3,19},{19,3},{4,20},{20... | collective-permute-start | bytes 786440 | tf_op jit(solution)/shard_map/ppermute | solution.py:155
  181.3 56.8 %collective-permute-start.7 = (bf16[512,256]{1,0:T(8,128)(2,1)S(1)}, bf16[512,256]{1,0:T(8,128)(2,1)S(1)}, u32[]{:S(2)}, u32[]{:S(2)}) collective-permute-start(bf16[512,256]{1,0:T(8,128)(2,1)S(1)} %convolution_convert_fusion.5), channel_id=1, source_target_pairs={{0,16},{16,0},{1,17},{17,1},{2,18},{18,2},{3,19},{19,3},{4,20},{20... | collective-permute-start | bytes 786440 | tf_op jit(solution)/shard_map/ppermute | solution.py:155
  182.8 35.7 %collective-permute-start.2 = (bf16[512,256]{1,0:T(8,128)(2,1)S(1)}, bf16[512,256]{1,0:T(8,128)(2,1)S(1)}, u32[]{:S(2)}, u32[]{:S(2)}) collective-permute-start(bf16[512,256]{1,0:T(8,128)(2,1)S(1)} %convolution_convert_fusion.10), channel_id=1, source_target_pairs={{0,16},{16,0},{1,17},{17,1},{2,18},{18,2},{3,19},{19,3},{4,20},{20... | collective-permute-start | bytes 786440 | tf_op jit(solution)/shard_map/ppermute | solution.py:155
  216.8 26.9 %collective-permute-start.9 = (bf16[512,256]{1,0:T(8,128)(2,1)S(1)}, bf16[512,256]{1,0:T(8,128)(2,1)S(1)}, u32[]{:S(2)}, u32[]{:S(2)}) collective-permute-start(bf16[512,256]{1,0:T(8,128)(2,1)S(1)} %convolution_convert_fusion.3), channel_id=1, source_target_pairs={{0,16},{16,0},{1,17},{17,1},{2,18},{18,2},{3,19},{19,3},{4,20},{20... | collective-permute-start | bytes 786440 | tf_op jit(solution)/shard_map/ppermute | solution.py:155
  218.5 13.1 %collective-permute-start.4 = (bf16[512,256]{1,0:T(8,128)(2,1)S(1)}, bf16[512,256]{1,0:T(8,128)(2,1)S(1)}, u32[]{:S(2)}, u32[]{:S(2)}) collective-permute-start(bf16[512,256]{1,0:T(8,128)(2,1)S(1)} %convolution_convert_fusion.8), channel_id=1, source_target_pairs={{0,16},{16,0},{1,17},{17,1},{2,18},{18,2},{3,19},{19,3},{4,20},{20... | collective-permute-start | bytes 786440 | tf_op jit(solution)/shard_map/ppermute | solution.py:155
  219.8 17.5 %collective-permute-start.6 = (bf16[512,256]{1,0:T(8,128)(2,1)S(1)}, bf16[512,256]{1,0:T(8,128)(2,1)S(1)}, u32[]{:S(2)}, u32[]{:S(2)}) collective-permute-start(bf16[512,256]{1,0:T(8,128)(2,1)S(1)} %convolution_convert_fusion.6), channel_id=1, source_target_pairs={{0,16},{16,0},{1,17},{17,1},{2,18},{18,2},{3,19},{19,3},{4,20},{20... | collective-permute-start | bytes 786440 | tf_op jit(solution)/shard_map/ppermute | solution.py:155
  231.6 11.2 %collective-permute-start.8 = (bf16[512,256]{1,0:T(8,128)(2,1)S(1)}, bf16[512,256]{1,0:T(8,128)(2,1)S(1)}, u32[]{:S(2)}, u32[]{:S(2)}) collective-permute-start(bf16[512,256]{1,0:T(8,128)(2,1)S(1)} %convolution_convert_fusion.4), channel_id=1, source_target_pairs={{0,16},{16,0},{1,17},{17,1},{2,18},{18,2},{3,19},{19,3},{4,20},{20... | collective-permute-start | bytes 786440 | tf_op jit(solution)/shard_map/ppermute | solution.py:155
  234.1 13.8 %collective-permute-start.10 = (bf16[512,256]{1,0:T(8,128)(2,1)S(1)}, bf16[512,256]{1,0:T(8,128)(2,1)S(1)}, u32[]{:S(2)}, u32[]{:S(2)}) collective-permute-start(bf16[512,256]{1,0:T(8,128)(2,1)S(1)} %convolution_convert_fusion.2), channel_id=1, source_target_pairs={{0,16},{16,0},{1,17},{17,1},{2,18},{18,2},{3,19},{19,3},{4,20},{20... | collective-permute-start | bytes 786440 | tf_op jit(solution)/shard_map/ppermute | solution.py:155
  247.9 1.9 copy-start.1
  248.8 1.1 copy-start.17

commit v3 on v2

--- a/solution.py
+++ b/solution.py
@@ -177,62 +177,96 @@
     return along_z, {"mp": index_of(z, 1 - y, core)}, {"mp": index_of(z, y, 1 - core)}
 
 
-def gather_kernel(from_partner, block_ref, out_ref, send_sem, recv_sem):
+def gather_kernel(
+    from_partner, block_ref, out_ref, x_send, up_send, down_send, y_send, core_send, recv_sem
+):
     me, z, y, core = place_of()
-    along_z, across_y, sibling = mp_peers()
+    _, across_y, sibling = mp_peers()
     partner = {"dp": 1 - lax.axis_index("dp")}
-    greet(along_z + [across_y, sibling] + ([partner] if from_partner else []))
-    started = []
-
-    def copy(source, slot, peer):
+    above = {"mp": index_of(lax.rem(z + 1, 4), y, core)}
+    below = {"mp": index_of(lax.rem(z + 3, 4), y, core)}
+    has_above, has_below = z < 3, z > 0
+    barrier = pltpu.get_barrier_semaphore()
+
+    def greet_one(peer):
+        pl.semaphore_signal(barrier, inc=1, device_id=peer, device_id_type=pl.DeviceIdType.MESH)
+
+    greet_one(across_y)
+    greet_one(sibling)
+    if from_partner:
+        greet_one(partner)
+    pl.when(has_above)(lambda: greet_one(above))
+    pl.when(has_below)(lambda: greet_one(below))
+    inner = has_above.astype(jnp.int32) + has_below.astype(jnp.int32)
+    pl.semaphore_wait(barrier, (3 if from_partner else 2) + inner)
+
+    def copy(slot, send_sem, peer, source=None):
         return pltpu.make_async_remote_copy(
-            src_ref=source,
+            src_ref=out_ref.at[slot] if source is None else source,
             dst_ref=out_ref.at[slot],
-            send_sem=send_sem.at[len(started)],
+            send_sem=send_sem,
             recv_sem=recv_sem.at[slot],
             device_id=peer,
             device_id_type=pl.DeviceIdType.MESH,
         )
 
-    def send(source, slot, peer):
-        one = copy(source, slot, peer)
-        one.start()
-        started.append(one)
-
-    def arrive(slot, peer):
-        pltpu.make_async_remote_copy(
-            src_ref=out_ref.at[slot],
-            dst_ref=out_ref.at[slot],
-            send_sem=send_sem.at[0],
-            recv_sem=recv_sem.at[slot],
-            device_id=peer,
-            device_id_type=pl.DeviceIdType.MESH,
-        ).wait_recv()
+    def column_slot(zz):
+        return index_of(zz, y, core)
+
+    def y_copy(zz):
+        return copy(column_slot(zz), y_send.at[zz], across_y)
+
+    def core_copy(zz, yy):
+        return copy(index_of(zz, yy, core), core_send.at[zz * 2 + yy], sibling)
+
+    def up_copy(step):
+        return copy(column_slot(z - step), up_send.at[step], above)
+
+    def down_copy(step):
+        return copy(column_slot(z + step), down_send.at[step], below)
 
     if from_partner:
-        send(block_ref, me, partner)
-        arrive(me, partner)
+        exchange = copy(me, x_send, partner, block_ref)
+        exchange.start()
+        exchange.wait()
     else:
         out_ref[me] = block_ref[...]
-    mine = out_ref.at[me]
-    for peer in along_z:
-        send(mine, me, peer)
-    send(mine, me, across_y)
-    send(mine, me, sibling)
+    pl.when(has_above)(lambda: up_copy(0).start())
+    pl.when(has_below)(lambda: down_copy(0).start())
+    y_copy(z).start()
+    core_copy(z, y).start()
     for step in (1, 2, 3):
-        slot = index_of(lax.rem(z + step, 4), y, core)
-        arrive(slot, along_z[step - 1])
-        send(out_ref.at[slot], slot, across_y)
-        send(out_ref.at[slot], slot, sibling)
+
+        @pl.when(z >= step)
+        def _():
+            copy(column_slot(z - step), y_send.at[0], below).wait_recv()
+            if step < 3:
+                pl.when(has_above)(lambda: up_copy(step).start())
+            y_copy(z - step).start()
+            core_copy(z - step, y).start()
+
+        @pl.when(z + step <= 3)
+        def _():
+            copy(column_slot(z + step), y_send.at[0], above).wait_recv()
+            if step < 3:
+                pl.when(has_below)(lambda: down_copy(step).start())
+            y_copy(z + step).start()
+            core_copy(z + step, y).start()
+
     for step in range(4):
-        slot = index_of(lax.rem(z + step, 4), 1 - y, core)
-        arrive(slot, across_y)
-        send(out_ref.at[slot], slot, sibling)
-    for step in range(4):
-        for row in (y, 1 - y):
-            arrive(index_of(lax.rem(z + step, 4), row, 1 - core), sibling)
-    for one in started:
-        one.wait_send()
+        zz = lax.rem(z + step, 4)
+        copy(index_of(zz, 1 - y, core), y_send.at[0], across_y).wait_recv()
+        core_copy(zz, 1 - y).start()
+    for zz in range(4):
+        for yy in range(2):
+            copy(index_of(zz, yy, 1 - core), y_send.at[0], sibling).wait_recv()
+    for step in (0, 1, 2):
+        pl.when(jnp.logical_and(has_above, z >= step))(lambda: up_copy(step).wait_send())
+        pl.when(jnp.logical_and(has_below, z + step <= 3))(lambda: down_copy(step).wait_send())
+    for zz in range(4):
+        y_copy(zz).wait_send()
+        for yy in range(2):
+            core_copy(zz, yy).wait_send()
 
 
 def gather_mp(block, from_partner, collective_id):
@@ -244,7 +278,11 @@
         in_specs=[pl.BlockSpec(memory_space=pltpu.VMEM)],
         out_specs=pl.BlockSpec(memory_space=pltpu.VMEM),
         scratch_shapes=[
-            pltpu.SemaphoreType.DMA((count,)),
+            pltpu.SemaphoreType.DMA(()),
+            pltpu.SemaphoreType.DMA((3,)),
+            pltpu.SemaphoreType.DMA((3,)),
+            pltpu.SemaphoreType.DMA((4,)),
+            pltpu.SemaphoreType.DMA((8,)),
             pltpu.SemaphoreType.DMA((count,)),
         ],
         compiler_params=pltpu.CompilerParams(
@@ -441,29 +479,39 @@
     own_rows, other_rows = split_rows(pre_local)
     partner_tokens = gather_mp(other_rows, True, 3)
     columns = gate_weight.shape[1]
-    width = 256
-    weights = []
-    parts = []
-    for start in range(0, columns, width):
-        pair = tuple(
-            weight[:, start : start + width].astype(bf16) for weight in (gate_weight, up_weight)
-        )
-        weights.append(pair)
-        parts.append(
-            tuple(
-                jnp.dot(partner_tokens, piece, preferred_element_type=jnp.float32).astype(bf16)
-                for piece in pair
-            )
-        )
+    width = columns // 2
+    early_weights = lax.optimization_barrier((gate_weight, up_weight, partner_tokens))[:2]
+    cuts = range(0, columns, width)
+    parts = [
+        tuple(
+            jnp.dot(
+                partner_tokens,
+                weight[:, start : start + width].astype(bf16),
+                preferred_element_type=jnp.float32,
+            ).astype(bf16)
+            for weight in early_weights
+        )
+        for start in cuts
+    ]
     own_rows = lax.optimization_barrier((parts, own_rows))[1]
     sent = [tuple(swap_dp(part) for part in pair) for pair in parts]
     own_tokens = gather_mp(own_rows, False, 4)
+    late_weights = lax.optimization_barrier((gate_weight, up_weight, own_tokens))[:2]
+    products = [
+        tuple(
+            jnp.dot(
+                own_tokens,
+                weight[:, start : start + width].astype(bf16),
+                preferred_element_type=jnp.float32,
+            )
+            for weight in late_weights
+        )
+        for start in cuts
+    ]
     hidden = []
-    for pair, arrived in zip(weights, sent):
+    for pair, arrived in zip(products, sent):
         gate, up_part = tuple(
-            jnp.dot(own_tokens, piece, preferred_element_type=jnp.float32)
-            + other.astype(jnp.float32)
-            for piece, other in zip(pair, arrived)
+            piece + other.astype(jnp.float32) for piece, other in zip(pair, arrived)
         )
         hidden.append((jax.nn.gelu(gate, approximate=True) * up_part).astype(bf16))
     return (residual, jnp.concatenate(hidden, axis=1), keys_rot, values_all)

time: 251 us -> 232 us (0.924)
  Pallas kernels: 156 us -> 131 us
  other arithmetic: 28.4 us -> 44.5 us
  waiting for transfers between devices: 21.8 us -> 12.6 us
  matrix products: 25.2 us -> 33.3 us
  starting transfers between devices: 11.4 us -> 4.98 us
    pallas_call x4, Pallas kernels: 113 us -> 91.8 us  [gather_mp(): pl.pallas_call(functools.partial(gather_kernel, from_partner), out_shape=...]
    another operation x6 -> x8, other arithmetic: 20 us -> 35.6 us
    ppermute x11 -> x5, waiting for transfers between devices: 21.8 us -> 12.6 us  [swap_dp(): return lax.ppermute(value, 'dp', [(0, 1), (1, 0)])]
    dot_general x20 -> x8, matrix products: 16.1 us -> 24.2 us  [the longest x4 12.2 us: on_device_pair(): jnp.dot(own_tokens, weight[:, start:start + width].astype(bf16), preferre...]
    ppermute x11 -> x5, starting transfers between devices: 11.4 us -> 4.98 us  [swap_dp(): return lax.ppermute(value, 'dp', [(0, 1), (1, 0)])]
    pallas_call x1, Pallas kernels: 42.9 us -> 39.3 us  [scatter_mp(): pl.pallas_call(scatter_kernel, out_shape=jax.ShapeDtypeStruct((rows, colu...]
  transfers between devices with their start and end apart: 11 -> 5, of which waited for: 4 -> 1; matrix products, arithmetic and copies ran while one was open for 10% -> 12% of each run, Pallas kernels for 22% -> 17%
where the time goes in v3:
time: 232 us; the launch traced here: 231 us
  Pallas kernels  131 us (56%)
  other arithmetic  44.5 us (19%)
  matrix products  33.3 us (14%)
  waiting for transfers between devices  12.6 us (5%)
  starting transfers between devices  4.98 us (2%)
  local copies, waits for them, and re-layouts  3.19 us (1%)
    pallas_call x4, Pallas kernels, gather_mp(): pl.pallas_call(functools.partial(gather_kernel, from_partner), out_shape=...  91.8 us
    pallas_call x1, Pallas kernels, scatter_mp(): pl.pallas_call(scatter_kernel, out_shape=jax.ShapeDtypeStruct((rows, colu...  39.3 us
    another operation x8, other arithmetic  35.6 us
    ppermute x5, waiting for transfers between devices, swap_dp(): return lax.ppermute(value, 'dp', [(0, 1), (1, 0)])  12.6 us
    dot_general x4, matrix products, on_device_pair(): jnp.dot(own_tokens, weight[:, start:start + width].astype(bf16), preferre...  12.2 us
    dot_general x4, matrix products, on_device_pair(): jnp.dot(partner_tokens, weight[:, start:start + width].astype(bf16), pref...  12 us
    ppermute x5, starting transfers between devices, swap_dp(): return lax.ppermute(value, 'dp', [(0, 1), (1, 0)])  4.98 us
  transfers between devices with their start and end apart: 5, of which 1 were waited for; matrix products, arithmetic and copies ran while one was open for 12% of the time, Pallas kernels for 17%

profile of v3, /device:TPU:0, one launch (start us, length us, event | category | flops | bytes accessed | tf_op | source)
XLA Modules:
  0.0 231.3 jit_solution(16747861533873509047)
XLA Ops:
  0.6 0.0 copy-start
  0.7 1.3 fusion.53
  2.0 2.2 convert.32
  4.2 2.2 convert.33
  6.4 1.1 convert.31
  7.6 0.1 fusion.55
  7.7 0.0 copy-start.7
  7.8 27.9 %shard_map.138 = bf16[16,32,2304]{2,1,0:T(8,128)(2,1)S(1)} custom-call(bf16[32,2304]{1,0:T(8,128)(2,1)S(1)} %get-tuple-element.25.block_ref), custom_call_target="tpu_custom_call" | custom-call | flops 15000000512 | bytes 10000000 | tf_op jit(solution)/shard_map/pallas_call | solution.py:275
  35.7 1.4 convolution_convert_fusion.1
  37.1 0.8 collective-permute-start
  38.6 19.9 %shard_map.139 = bf16[16,32,2304]{2,1,0:T(8,128)(2,1)S(1)} custom-call(bf16[32,2304]{1,0:T(8,128)(2,1)S(1)} %get-tuple-element.10.block_ref), custom_call_target="tpu_custom_call" | custom-call | flops 15000000512 | bytes 10000000 | tf_op jit(solution)/shard_map/pallas_call | solution.py:275
  58.5 0.8 fusion.48
  59.3 1.7 multiply_cosine_fusion
  61.1 1.4 convert_add_fusion
  62.5 0.9 slice.72
  63.4 0.2 copy-done.10
  63.6 1.8 fusion.61
  65.5 1.3 reshape.209
  66.8 0.6 fusion.76
  67.4 1.2 fusion.63
  68.6 0.1 subtract_convert_fusion
  68.8 2.2 bitcast_select_fusion
  71.0 2.7 %fusion.46 = bf16[128,2,512]{2,0,1:T(8,128)(2,1)S(1)} fusion(f32[2,512,512]{1,2,0:T(8,128)} %bitcast_select_fusion, pred[512]{0:T(512)(128)(4,1)S(1)} %iota_compare_fusion.1, bf16[512,128]{1,0:T(8,128)(2,1)S(1)} %get-tuple-element.30), kind=kOutput, calls=%fused_computation.47 | convolution fusion | flops 135529984 | bytes 2490880 | tf_op jit(solution)/shard_map/hqk,kd->qhd/dot_general | solution.py:61
  73.7 1.4 convolution_convert_fusion
  75.2 39.3 %shard_map.140 = f32[32,4608]{1,0:T(8,128)S(1)} custom-call(bf16[16,32,4608]{2,1,0:T(8,128)(2,1)S(1)} %bitcast.39), custom_call_target="tpu_custom_call" | custom-call | flops 30000001024 | bytes 10000000 | tf_op jit(solution)/shard_map/pallas_call | solution.py:399
  114.5 0.2 multiply_reduce_fusion
  114.6 0.3 fusion.50
  115.0 0.1 fusion.52
  115.2 24.3 %shard_map.141 = bf16[16,32,2304]{2,1,0:T(8,128)(2,1)S(1)} custom-call(bf16[32,2304]{1,0:T(8,128)(2,1)S(1)} %get-tuple-element.23.block_ref), custom_call_target="tpu_custom_call" | custom-call | flops 15000000512 | bytes 10000000 | tf_op jit(solution)/shard_map/pallas_call | solution.py:275
  139.5 7.5 %convert.36 = bf16[2304,1280]{1,0:T(8,128)(2,1)} convert(f32[2304,1280]{1,0:T(8,128)} %param.20) | non-fusion elementwise | flops 2949120 | bytes 17694720 | tf_op jit(solution)/shard_map/convert.7
  147.0 4.0 %fusion.22 = bf16[512,640]{1,0:T(8,128)(2,1)S(1)} fusion(bf16[512,2304]{1,0:T(8,128)(2,1)S(1)} %bitcast.45, bf16[2304,1280]{1,0:T(8,128)(2,1)} %convert.36), kind=kOutput, calls=%fused_computation.24 | convolution fusion | flops 1510277120 | bytes 5963776 | tf_op jit(solution)/shard_map/dot_general | solution.py:487
  151.0 2.0 fusion.16
  153.0 7.5 %convert.37 = bf16[2304,1280]{1,0:T(8,128)(2,1)} convert(f32[2304,1280]{1,0:T(8,128)} %param.21) | non-fusion elementwise | flops 2949120 | bytes 17694720 | tf_op jit(solution)/shard_map/convert.6
  160.5 4.0 %fusion.25 = bf16[512,640]{1,0:T(8,128)(2,1)S(1)} fusion(bf16[512,2304]{1,0:T(8,128)(2,1)S(1)} %bitcast.47, bf16[2304,1280]{1,0:T(8,128)(2,1)} %convert.37), kind=kOutput, calls=%fused_computation.25 | convolution fusion | flops 1510277120 | bytes 5963776 | tf_op jit(solution)/shard_map/dot_general | solution.py:487
  164.5 2.0 fusion.19
  166.5 0.8 collective-permute-start.1
  167.3 1.3 collective-permute-start.3
  168.6 0.7 collective-permute-start.2
  169.3 1.3 collective-permute-start.4
  170.6 19.7 %shard_map.142 = bf16[16,32,2304]{2,1,0:T(8,128)(2,1)S(1)} custom-call(bf16[32,2304]{1,0:T(8,128)(2,1)S(1)} %get-tuple-element.13.block_ref), custom_call_target="tpu_custom_call" | custom-call | flops 15000000512 | bytes 10000000 | tf_op jit(solution)/shard_map/pallas_call | solution.py:275
  190.3 7.5 %convert.38 = bf16[2304,1280]{1,0:T(8,128)(2,1)} convert(f32[2304,1280]{1,0:T(8,128)} %param.20) | non-fusion elementwise | flops 2949120 | bytes 17694720 | tf_op jit(solution)/shard_map/convert.3
  197.7 3.8 %fusion.2 = f32[512,640]{1,0:T(8,128)S(1)} fusion(bf16[512,2304]{1,0:T(8,128)(2,1)S(1)} %bitcast.40, bf16[2304,1280]{1,0:T(8,128)(2,1)} %convert.38), kind=kOutput, calls=%fused_computation.3 | convolution fusion | flops 1509949440 | bytes 6619136 | tf_op jit(solution)/shard_map/dot_general | solution.py:502
  201.6 7.5 %convert.39 = bf16[2304,1280]{1,0:T(8,128)(2,1)} convert(f32[2304,1280]{1,0:T(8,128)} %param.21) | non-fusion elementwise | flops 2949120 | bytes 17694720 | tf_op jit(solution)/shard_map/convert.2
  209.1 4.0 %fusion.6 = f32[512,640]{1,0:T(8,128)S(1)} fusion(bf16[512,2304]{1,0:T(8,128)(2,1)S(1)} %bitcast.41, bf16[2304,1280]{1,0:T(8,128)(2,1)} %convert.38), kind=kOutput, calls=%fused_computation.7 | convolution fusion | flops 1509949440 | bytes 6619136 | tf_op jit(solution)/shard_map/dot_general | solution.py:502
  213.1 12.6 %collective-permute-done.4 = bf16[512,640]{1,0:T(8,128)(2,1)S(1)} collective-permute-done((bf16[512,640]{1,0:T(8,128)(2,1)S(1)}, bf16[512,640]{1,0:T(8,128)(2,1)S(1)}, u32[]{:S(2)}, u32[]{:S(2)}) %collective-permute-start.4) | collective-permute-done | bytes 655392 | tf_op jit(solution)/shard_map/ppermute | solution.py:155
  225.7 2.2 fusion.45
  227.9 2.2 fusion.36
  230.1 1.2 pad_maximum_fusion.1
  (48 shorter events, 0.2 us)
Async XLA Ops:
  0.6 73.1 %copy-start = (bf16[256,4608]{1,0:T(8,128)(2,1)S(1)}, bf16[256,4608]{1,0:T(8,128)(2,1)}, u32[]{:S(2)}) copy-start(bf16[256,4608]{1,0:T(8,128)(2,1)} %param.17) | copy-start | bytes 7077892
  0.7 5.8 %copy-start.6 = (f32[2304,256]{1,0:T(8,128)S(1)}, f32[2304,256]{1,0:T(8,128)}, u32[]{:S(2)}) copy-start(f32[2304,256]{1,0:T(8,128)} %param.14) | copy-start | bytes 7077892
  4.2 3.3 %copy-start.5 = (bf16[32,4608]{1,0:T(8,128)(2,1)S(1)}, bf16[32,4608]{1,0:T(8,128)(2,1)}, u32[]{:S(2)}) copy-start(bf16[32,4608]{1,0:T(8,128)(2,1)} %param.11) | copy-start | bytes 884740
  4.2 3.3 %copy-start.16 = (f32[4608]{0:T(1024)S(1)}, f32[4608]{0:T(1024)}, u32[]{:S(2)}) copy-start(f32[4608]{0:T(1024)} %param.13) | copy-start | bytes 55300
  7.7 27.9 %copy-start.7 = (bf16[2304,256]{1,0:T(8,128)(2,1)S(1)}, bf16[2304,256]{1,0:T(8,128)(2,1)}, u32[]{:S(2)}) copy-start(bf16[2304,256]{1,0:T(8,128)(2,1)} %convert.31) | copy-start | bytes 3538948
  7.7 27.9 %copy-start.11 = (bf16[2304,128]{1,0:T(8,128)(2,1)S(1)}, bf16[2304,128]{1,0:T(8,128)(2,1)}, u32[]{:S(2)}) copy-start(bf16[2304,128]{1,0:T(8,128)(2,1)} %convert.32) | copy-start | bytes 1769476
  7.8 27.9 %copy-start.12 = (bf16[2304,128]{1,0:T(8,128)(2,1)S(1)}, bf16[2304,128]{1,0:T(8,128)(2,1)}, u32[]{:S(2)}) copy-start(bf16[2304,128]{1,0:T(8,128)(2,1)} %convert.33) | copy-start | bytes 1769476
  37.1 24.0 %collective-permute-start = (bf16[512,512]{1,0:T(8,128)(2,1)S(1)}, bf16[512,512]{1,0:T(8,128)(2,1)S(1)}, u32[]{:S(2)}, u32[]{:S(2)}) collective-permute-start(bf16[512,512]{1,0:T(8,128)(2,1)S(1)} %convolution_convert_fusion.1), channel_id=1, source_target_pairs={{0,16},{16,0},{1,17},{17,1},{2,18},{18,2},{3,19},{19,3},{4,20},{20... | collective-permute-start | bytes 1572872 | tf_op jit(solution)/shard_map/ppermute | solution.py:155
  62.5 1.1 copy-start.10
  66.8 1.9 copy-start.9
  66.8 2.0 copy-start.13
  68.6 2.4 %copy-start.15 = (bf16[512,128]{1,0:T(8,128)(2,1)}, bf16[512,128]{1,0:T(8,128)(2,1)S(1)}, u32[]{:S(2)}) copy-start(bf16[512,128]{1,0:T(8,128)(2,1)S(1)} %get-tuple-element.31) | copy-start | bytes 393220
  68.6 2.4 %copy-start.14 = (bf16[512,128]{1,0:T(8,128)(2,1)}, bf16[512,128]{1,0:T(8,128)(2,1)S(1)}, u32[]{:S(2)}) copy-start(bf16[512,128]{1,0:T(8,128)(2,1)S(1)} %get-tuple-element.30) | copy-start | bytes 393220
  75.2 39.5 %copy-start.18 = (f32[4608]{0:T(1024)S(1)}, f32[4608]{0:T(1024)}, u32[]{:S(2)}) copy-start(f32[4608]{0:T(1024)} %param.18) | copy-start | bytes 55300
  75.2 39.8 %copy-start.17 = (f32[4608]{0:T(1024)S(1)}, f32[4608]{0:T(1024)}, u32[]{:S(2)}) copy-start(f32[4608]{0:T(1024)} %param.19) | copy-start | bytes 55300
  114.9 24.6 %copy-start.8 = (bf16[32,4608]{1,0:T(8,128)(2,1)}, bf16[32,4608]{1,0:T(8,128)(2,1)S(1)}, u32[]{:S(2)}) copy-start(bf16[32,4608]{1,0:T(8,128)(2,1)S(1)} %get-tuple-element.17) | copy-start | bytes 884740
  147.0 4.0 %copy-start.4 = (bf16[2304,1280]{1,0:T(8,128)(2,1)S(1)}, bf16[2304,1280]{1,0:T(8,128)(2,1)}, u32[]{:S(2)}) copy-start(bf16[2304,1280]{1,0:T(8,128)(2,1)} %convert.36) | copy-start | bytes 17694724
  160.5 4.0 %copy-start.3 = (bf16[2304,1280]{1,0:T(8,128)(2,1)S(1)}, bf16[2304,1280]{1,0:T(8,128)(2,1)}, u32[]{:S(2)}) copy-start(bf16[2304,1280]{1,0:T(8,128)(2,1)} %convert.37) | copy-start | bytes 17694724
  166.5 61.4 %collective-permute-start.1 = (bf16[512,640]{1,0:T(8,128)(2,1)S(1)}, bf16[512,640]{1,0:T(8,128)(2,1)S(1)}, u32[]{:S(2)}, u32[]{:S(2)}) collective-permute-start(bf16[512,640]{1,0:T(8,128)(2,1)S(1)} %fusion.16), channel_id=1, source_target_pairs={{0,16},{16,0},{1,17},{17,1},{2,18},{18,2},{3,19},{19,3},{4,20},{20... | collective-permute-start | bytes 1966088 | tf_op jit(solution)/shard_map/ppermute | solution.py:155
  167.3 45.7 %collective-permute-start.3 = (bf16[512,640]{1,0:T(8,128)(2,1)S(1)}, bf16[512,640]{1,0:T(8,128)(2,1)S(1)}, u32[]{:S(2)}, u32[]{:S(2)}) collective-permute-start(bf16[512,640]{1,0:T(8,128)(2,1)S(1)} %fusion.22), channel_id=1, source_target_pairs={{0,16},{16,0},{1,17},{17,1},{2,18},{18,2},{3,19},{19,3},{4,20},{20... | collective-permute-start | bytes 1966088 | tf_op jit(solution)/shard_map/ppermute | solution.py:155
  168.6 59.3 %collective-permute-start.2 = (bf16[512,640]{1,0:T(8,128)(2,1)S(1)}, bf16[512,640]{1,0:T(8,128)(2,1)S(1)}, u32[]{:S(2)}, u32[]{:S(2)}) collective-permute-start(bf16[512,640]{1,0:T(8,128)(2,1)S(1)} %fusion.19), channel_id=1, source_target_pairs={{0,16},{16,0},{1,17},{17,1},{2,18},{18,2},{3,19},{19,3},{4,20},{20... | collective-permute-start | bytes 1966088 | tf_op jit(solution)/shard_map/ppermute | solution.py:155
  169.3 56.4 %collective-permute-start.4 = (bf16[512,640]{1,0:T(8,128)(2,1)S(1)}, bf16[512,640]{1,0:T(8,128)(2,1)S(1)}, u32[]{:S(2)}, u32[]{:S(2)}) collective-permute-start(bf16[512,640]{1,0:T(8,128)(2,1)S(1)} %fusion.25), channel_id=1, source_target_pairs={{0,16},{16,0},{1,17},{17,1},{2,18},{18,2},{3,19},{19,3},{4,20},{20... | collective-permute-start | bytes 1966088 | tf_op jit(solution)/shard_map/ppermute | solution.py:155
  209.1 16.6 %copy-start.2 = (bf16[2304,1280]{1,0:T(8,128)(2,1)S(1)}, bf16[2304,1280]{1,0:T(8,128)(2,1)}, u32[]{:S(2)}) copy-start(bf16[2304,1280]{1,0:T(8,128)(2,1)} %convert.39) | copy-start | bytes 17694724
  227.9 3.4 %copy-start.1 = (bf16[256,4608]{1,0:T(8,128)(2,1)S(1)}, bf16[256,4608]{1,0:T(8,128)(2,1)}, u32[]{:S(2)}) copy-start(bf16[256,4608]{1,0:T(8,128)(2,1)} %param.17) | copy-start | bytes 7077892

commit v4 on v3

--- a/solution.py
+++ b/solution.py
@@ -288,7 +288,7 @@
         compiler_params=pltpu.CompilerParams(
             collective_id=collective_id, has_side_effects=True, vmem_limit_bytes=32 * 2**20
         ),
-        cost_estimate=pl.CostEstimate(flops=15 * 10**9, bytes_accessed=10**7, transcendentals=0),
+        cost_estimate=pl.CostEstimate(flops=10**9, bytes_accessed=10**6, transcendentals=0),
     )(block)
     return out.reshape(count * rows, columns)
 
@@ -417,6 +417,34 @@
         ),
         cost_estimate=pl.CostEstimate(flops=30 * 10**9, bytes_accessed=10**7, transcendentals=0),
     )(partial.reshape(count, rows, columns))
+
+
+def project_kernel(tokens_ref, weight_ref, out_ref):
+    out_ref[...] = jnp.dot(
+        tokens_ref[...], weight_ref[...].astype(jnp.bfloat16), preferred_element_type=jnp.float32
+    ).astype(out_ref.dtype)
+
+
+def project(tokens, weight, dtype):
+    count, depth = tokens.shape
+    columns = weight.shape[1]
+    width = 256
+    return pl.pallas_call(
+        project_kernel,
+        grid=(columns // width,),
+        out_shape=jax.ShapeDtypeStruct((count, columns), dtype),
+        in_specs=[
+            pl.BlockSpec((count, depth), lambda i: (0, 0)),
+            pl.BlockSpec((depth, width), lambda i: (0, i)),
+        ],
+        out_specs=pl.BlockSpec((count, width), lambda i: (0, i)),
+        compiler_params=pltpu.CompilerParams(vmem_limit_bytes=32 * 2**20),
+        cost_estimate=pl.CostEstimate(
+            flops=2 * count * depth * columns,
+            bytes_accessed=4 * depth * columns + 2 * count * (depth + columns),
+            transcendentals=0,
+        ),
+    )(tokens, weight)
 
 
 def split_rows(block):
@@ -478,43 +506,17 @@
     pre_local = rms_norm(residual.astype(jnp.float32), gain_pre).astype(bf16)
     own_rows, other_rows = split_rows(pre_local)
     partner_tokens = gather_mp(other_rows, True, 3)
-    columns = gate_weight.shape[1]
-    width = columns // 2
-    early_weights = lax.optimization_barrier((gate_weight, up_weight, partner_tokens))[:2]
-    cuts = range(0, columns, width)
-    parts = [
-        tuple(
-            jnp.dot(
-                partner_tokens,
-                weight[:, start : start + width].astype(bf16),
-                preferred_element_type=jnp.float32,
-            ).astype(bf16)
-            for weight in early_weights
-        )
-        for start in cuts
-    ]
-    own_rows = lax.optimization_barrier((parts, own_rows))[1]
-    sent = [tuple(swap_dp(part) for part in pair) for pair in parts]
+    gate_part = project(partner_tokens, gate_weight, bf16)
+    gate_sent = swap_dp(gate_part)
+    up_tokens = lax.optimization_barrier((partner_tokens, gate_part))[0]
+    up_part = project(up_tokens, up_weight, bf16)
+    up_sent = swap_dp(up_part)
+    own_rows = lax.optimization_barrier((own_rows, up_part))[0]
     own_tokens = gather_mp(own_rows, False, 4)
-    late_weights = lax.optimization_barrier((gate_weight, up_weight, own_tokens))[:2]
-    products = [
-        tuple(
-            jnp.dot(
-                own_tokens,
-                weight[:, start : start + width].astype(bf16),
-                preferred_element_type=jnp.float32,
-            )
-            for weight in late_weights
-        )
-        for start in cuts
-    ]
-    hidden = []
-    for pair, arrived in zip(products, sent):
-        gate, up_part = tuple(
-            piece + other.astype(jnp.float32) for piece, other in zip(pair, arrived)
-        )
-        hidden.append((jax.nn.gelu(gate, approximate=True) * up_part).astype(bf16))
-    return (residual, jnp.concatenate(hidden, axis=1), keys_rot, values_all)
+    gate = project(own_tokens, gate_weight, jnp.float32) + gate_sent.astype(jnp.float32)
+    up = project(own_tokens, up_weight, jnp.float32) + up_sent.astype(jnp.float32)
+    hidden = (jax.nn.gelu(gate, approximate=True) * up).astype(bf16)
+    return (residual, hidden, keys_rot, values_all)
 
 
 def solution(mesh):

time: 232 us -> 218 us (0.940)
  other arithmetic: 44.5 us -> 16.6 us
  matrix products: 33.3 us -> 9.08 us
  Pallas kernels: 131 us -> 152 us
  local copies, waits for them, and re-layouts: 3.19 us -> 16.5 us
  waiting for transfers between devices: 12.6 us -> 19 us
    another operation x8 -> x4, other arithmetic: 35.6 us -> 4.88 us
    dot_general x8 -> x0, matrix products: 24.2 us -> none  [the longest x4 12.2 us: on_device_pair(): jnp.dot(own_tokens, weight[:, start:start + width].astype(bf16), preferre...]
    pallas_call x0 -> x4, Pallas kernels: none -> 20.6 us  [project(): pl.pallas_call(project_kernel, grid=(columns // width,), out_shape=jax.Sh...]
    unnamed x38 -> x46, local copies, waits for them, and re-layouts: 0.27 us -> 13.5 us
    ppermute x5 -> x3, waiting for transfers between devices: 12.6 us -> 19 us  [swap_dp(): return lax.ppermute(value, 'dp', [(0, 1), (1, 0)])]
    convert_element_type x0 -> x1, other arithmetic: none -> 4.02 us  [on_device_pair(): hidden = (jax.nn.gelu(gate, approximate=True) * up).astype(bf16)]
    ppermute x5 -> x3, starting transfers between devices: 4.98 us -> 2.89 us  [swap_dp(): return lax.ppermute(value, 'dp', [(0, 1), (1, 0)])]
  transfers between devices with their start and end apart: 5 -> 3, of which waited for: 1 -> 1; matrix products, arithmetic and copies ran while one was open for 12% -> 1% of each run, Pallas kernels for 17% -> 23%
where the time goes in v4:
time: 218 us; the launch traced here: 217 us
  Pallas kernels  152 us (70%)
  waiting for transfers between devices  19 us (9%)
  other arithmetic  16.6 us (8%)
  local copies, waits for them, and re-layouts  16.5 us (8%)
  matrix products  9.08 us (4%)
  starting transfers between devices  2.89 us (1%)
    pallas_call x4, Pallas kernels, gather_mp(): pl.pallas_call(functools.partial(gather_kernel, from_partner), out_shape=...  91.7 us
    pallas_call x1, Pallas kernels, scatter_mp(): pl.pallas_call(scatter_kernel, out_shape=jax.ShapeDtypeStruct((rows, colu...  39.3 us
    pallas_call x4, Pallas kernels, project(): pl.pallas_call(project_kernel, grid=(columns // width,), out_shape=jax.Sh...  20.6 us
    ppermute x3, waiting for transfers between devices, swap_dp(): return lax.ppermute(value, 'dp', [(0, 1), (1, 0)])  19 us
    unnamed x46, local copies, waits for them, and re-layouts  13.5 us
    another operation x4, other arithmetic  4.88 us
  transfers between devices with their start and end apart: 3, of which 1 were waited for; matrix products, arithmetic and copies ran while one was open for 1% of the time, Pallas kernels for 23%

profile of v4, /device:TPU:0, one launch (start us, length us, event | category | flops | bytes accessed | tf_op | source)
XLA Modules:
  0.0 217.4 jit_solution(14985731794477334814)
XLA Ops:
  0.6 0.0 copy-start
  0.7 1.3 fusion.16
  2.0 1.4 convert.16
  3.4 0.0 copy-start.7
  3.4 0.0 copy-start.17
  3.4 2.2 %convert.17 = bf16[2304,128]{1,0:T(8,128)(2,1)} convert(f32[2304,128]{1,0:T(8,128)} %param.16) | non-fusion elementwise | flops 294912 | bytes 1769472 | tf_op jit(solution)/shard_map/convert.4
  5.6 1.1 convert.15
  6.7 0.1 fusion.18
  6.9 27.9 %shard_map.138 = bf16[16,32,2304]{2,1,0:T(8,128)(2,1)S(1)} custom-call(bf16[32,2304]{1,0:T(8,128)(2,1)S(1)} %get-tuple-element.19.block_ref), custom_call_target="tpu_custom_call" | custom-call | flops 1000000000 | bytes 1000000 | tf_op jit(solution)/shard_map/pallas_call | solution.py:275
  34.8 1.4 convolution_convert_fusion.1
  36.2 0.8 collective-permute-start
  37.7 19.9 %shard_map.139 = bf16[16,32,2304]{2,1,0:T(8,128)(2,1)S(1)} custom-call(bf16[32,2304]{1,0:T(8,128)(2,1)S(1)} %get-tuple-element.7.block_ref), custom_call_target="tpu_custom_call" | custom-call | flops 1000000000 | bytes 1000000 | tf_op jit(solution)/shard_map/pallas_call | solution.py:275
  57.6 0.8 fusion.11
  58.5 1.7 multiply_cosine_fusion
  60.2 1.4 convert_add_fusion
  61.6 0.0 copy-start.12
  61.7 0.9 slice.32
  62.6 0.2 copy-done.12
  62.8 1.8 fusion.24
  64.6 1.3 reshape.209
  65.9 0.6 fusion.39
  66.5 1.2 fusion.26
  67.8 0.0 copy-start.16
  67.8 0.0 copy-start.15
  67.8 0.1 subtract_convert_fusion
  68.0 2.2 %bitcast_select_fusion = f32[2,512,512]{1,2,0:T(8,128)} fusion(pred[512,512]{0,1:T(8,128)(4,1)S(1)} %copy-done.14, bf16[512,2,64]{2,0,1:T(8,128)(2,1)S(1)} %get-tuple-element.13, bf16[512,2,64]{2,0,1:T(8,128)(2,1)S(1)} %get-tuple-element.12, bf16[512,128]{1,0:T(8,128)(2,1)S(1)} %get-tuple-element.25), kind=kOutput, calls=%fused_computation.12 | convolution fusion | flops 136314880 | bytes 2752512 | tf_op jit(solution)/shard_map/qhd,kd->hqk/dot_general | solution.py:52
  70.2 2.7 %fusion.9 = bf16[128,2,512]{2,0,1:T(8,128)(2,1)S(1)} fusion(f32[2,512,512]{1,2,0:T(8,128)} %bitcast_select_fusion, pred[512]{0:T(512)(128)(4,1)S(1)} %iota_compare_fusion.1, bf16[512,128]{1,0:T(8,128)(2,1)S(1)} %get-tuple-element.24), kind=kOutput, calls=%fused_computation.16 | convolution fusion | flops 135529984 | bytes 2490880 | tf_op jit(solution)/shard_map/hqk,kd->qhd/dot_general | solution.py:61
  72.9 1.4 convolution_convert_fusion
  74.3 39.3 %shard_map.140 = f32[32,4608]{1,0:T(8,128)S(1)} custom-call(bf16[16,32,4608]{2,1,0:T(8,128)(2,1)S(1)} %bitcast.37), custom_call_target="tpu_custom_call" | custom-call | flops 30000001024 | bytes 10000000 | tf_op jit(solution)/shard_map/pallas_call | solution.py:399
  113.6 0.2 multiply_reduce_fusion
  113.8 0.0 slice-start
  113.8 0.3 fusion.13
  114.1 0.1 fusion.15
  114.3 24.3 %shard_map.141 = bf16[16,32,2304]{2,1,0:T(8,128)(2,1)S(1)} custom-call(bf16[32,2304]{1,0:T(8,128)(2,1)S(1)} %get-tuple-element.16.block_ref), custom_call_target="tpu_custom_call" | custom-call | flops 1000000000 | bytes 1000000 | tf_op jit(solution)/shard_map/pallas_call | solution.py:275
  138.7 4.3 %copy-done.2 = f32[2304,1280]{1,0:T(8,128)S(1)} copy-done((f32[2304,1280]{1,0:T(8,128)S(1)}, f32[2304,1280]{1,0:T(8,128)}, u32[]{:S(2)}) %copy-start.2) | copy-done | bytes 11796504
  143.0 5.5 %shard_map.142 = bf16[512,1280]{1,0:T(8,128)(2,1)} custom-call(bf16[512,2304]{1,0:T(8,128)(2,1)S(1)} %bitcast.35, f32[2304,1280]{1,0:T(8,128)S(1)} %copy-done.2), custom_call_target="tpu_custom_call" | custom-call | flops 3019898880 | bytes 15466496 | tf_op jit(solution)/shard_map/pallas_call | solution.py:432
  148.5 5.5 %shard_map.143 = bf16[512,1280]{1,0:T(8,128)(2,1)} custom-call(bf16[512,2304]{1,0:T(8,128)(2,1)S(1)} %bitcast.36, f32[2304,1280]{1,0:T(8,128)S(1)} %bitcast.32), custom_call_target="tpu_custom_call" | custom-call | flops 3019898880 | bytes 15466496 | tf_op jit(solution)/shard_map/pallas_call | solution.py:432
  154.0 0.8 collective-permute-start.2
  154.7 1.3 collective-permute-start.1
  156.0 19.7 %shard_map.144 = bf16[16,32,2304]{2,1,0:T(8,128)(2,1)S(1)} custom-call(bf16[32,2304]{1,0:T(8,128)(2,1)S(1)} %get-tuple-element.9.block_ref), custom_call_target="tpu_custom_call" | custom-call | flops 1000000000 | bytes 1000000 | tf_op jit(solution)/shard_map/pallas_call | solution.py:275
  175.7 4.8 %shard_map.146 = f32[512,1280]{1,0:T(8,128)S(1)} custom-call(bf16[512,2304]{1,0:T(8,128)(2,1)S(1)} %bitcast.33, f32[2304,1280]{1,0:T(8,128)S(1)} %bitcast.32), custom_call_target="tpu_custom_call" | custom-call | flops 3019898880 | bytes 15466496 | tf_op jit(solution)/shard_map/pallas_call | solution.py:432
  180.6 1.5 copy-done.4
  182.0 1.4 copy-done.5
  183.5 4.3 %copy-done.3 = f32[2304,1280]{1,0:T(8,128)S(1)} copy-done((f32[2304,1280]{1,0:T(8,128)S(1)}, f32[2304,1280]{1,0:T(8,128)}, u32[]{:S(2)}) %copy-start.3) | copy-done | bytes 11796504
  187.8 1.7 copy-done.6
  189.5 4.8 %shard_map.145 = f32[512,1280]{1,0:T(8,128)S(1)} custom-call(bf16[512,2304]{1,0:T(8,128)(2,1)S(1)} %bitcast.34, f32[2304,1280]{1,0:T(8,128)S(1)} %copy-done.3), custom_call_target="tpu_custom_call" | custom-call | flops 3019898880 | bytes 15466496 | tf_op jit(solution)/shard_map/pallas_call | solution.py:432
  194.3 19.0 %collective-permute-done.1 = bf16[512,1280]{1,0:T(8,128)(2,1)S(1)} collective-permute-done((bf16[512,1280]{1,0:T(8,128)(2,1)}, bf16[512,1280]{1,0:T(8,128)(2,1)S(1)}, u32[]{:S(2)}, u32[]{:S(2)}) %collective-permute-start.1) | collective-permute-done | bytes 1310752 | tf_op jit(solution)/shard_map/ppermute | solution.py:155
  213.3 4.0 %fusion.8 = bf16[512,1280]{1,0:T(8,128)(2,1)} fusion(f32[512,1280]{1,0:T(8,128)} %copy-done.4, bf16[512,1280]{1,0:T(8,128)(2,1)S(1)} %collective-permute-done.2, f32[512,1280]{1,0:T(8,128)S(1)} %shard_map.145, bf16[512,1280]{1,0:T(8,128)(2,1)S(1)} %collective-permute-done.1), kind=kLoop, calls=%fused_computation.10 | loop fusion | flops 9175040 | bytes 9175040 | tf_op jit(solution)/shard_map/convert_element_type | solution.py:518
  (45 shorter events, 0.2 us)
Async XLA Ops:
  0.6 72.2 %copy-start = (bf16[256,4608]{1,0:T(8,128)(2,1)S(1)}, bf16[256,4608]{1,0:T(8,128)(2,1)}, u32[]{:S(2)}) copy-start(bf16[256,4608]{1,0:T(8,128)(2,1)} %param.17) | copy-start | bytes 7077892
  0.7 5.0 %copy-start.8 = (f32[2304,256]{1,0:T(8,128)S(1)}, f32[2304,256]{1,0:T(8,128)}, u32[]{:S(2)}) copy-start(f32[2304,256]{1,0:T(8,128)} %param.14) | copy-start | bytes 7077892
  3.4 3.4 %copy-start.7 = (bf16[32,4608]{1,0:T(8,128)(2,1)S(1)}, bf16[32,4608]{1,0:T(8,128)(2,1)}, u32[]{:S(2)}) copy-start(bf16[32,4608]{1,0:T(8,128)(2,1)} %param.11) | copy-start | bytes 884740
  3.4 3.4 %copy-start.17 = (f32[4608]{0:T(1024)S(1)}, f32[4608]{0:T(1024)}, u32[]{:S(2)}) copy-start(f32[4608]{0:T(1024)} %param.13) | copy-start | bytes 55300
  6.7 28.1 %copy-start.9 = (bf16[2304,256]{1,0:T(8,128)(2,1)S(1)}, bf16[2304,256]{1,0:T(8,128)(2,1)}, u32[]{:S(2)}) copy-start(bf16[2304,256]{1,0:T(8,128)(2,1)} %convert.15) | copy-start | bytes 3538948
  6.7 28.1 %copy-start.13 = (bf16[2304,128]{1,0:T(8,128)(2,1)S(1)}, bf16[2304,128]{1,0:T(8,128)(2,1)}, u32[]{:S(2)}) copy-start(bf16[2304,128]{1,0:T(8,128)(2,1)} %convert.17) | copy-start | bytes 1769476
  36.2 24.0 %collective-permute-start = (bf16[512,512]{1,0:T(8,128)(2,1)S(1)}, bf16[512,512]{1,0:T(8,128)(2,1)S(1)}, u32[]{:S(2)}, u32[]{:S(2)}) collective-permute-start(bf16[512,512]{1,0:T(8,128)(2,1)S(1)} %convolution_convert_fusion.1), channel_id=1, source_target_pairs={{0,16},{16,0},{1,17},{17,1},{2,18},{18,2},{3,19},{19,3},{4,20},{20... | collective-permute-start | bytes 1572872 | tf_op jit(solution)/shard_map/ppermute | solution.py:155
  61.6 1.1 copy-start.12
  65.9 1.9 copy-start.11
  65.9 2.0 copy-start.14
  67.8 2.4 %copy-start.16 = (bf16[512,128]{1,0:T(8,128)(2,1)}, bf16[512,128]{1,0:T(8,128)(2,1)S(1)}, u32[]{:S(2)}) copy-start(bf16[512,128]{1,0:T(8,128)(2,1)S(1)} %get-tuple-element.25) | copy-start | bytes 393220
  67.8 2.4 %copy-start.15 = (bf16[512,128]{1,0:T(8,128)(2,1)}, bf16[512,128]{1,0:T(8,128)(2,1)S(1)}, u32[]{:S(2)}) copy-start(bf16[512,128]{1,0:T(8,128)(2,1)S(1)} %get-tuple-element.24) | copy-start | bytes 393220
  74.3 39.5 %copy-start.19 = (f32[4608]{0:T(1024)S(1)}, f32[4608]{0:T(1024)}, u32[]{:S(2)}) copy-start(f32[4608]{0:T(1024)} %param.18) | copy-start | bytes 55300
  74.3 39.8 %copy-start.18 = (f32[4608]{0:T(1024)S(1)}, f32[4608]{0:T(1024)}, u32[]{:S(2)}) copy-start(f32[4608]{0:T(1024)} %param.19) | copy-start | bytes 55300
  113.8 34.7 %slice-start = ((s8[11796480]{0:T(1024)(128)(4,1)}), s8[4194304]{0:T(1024)(128)(4,1)S(1)}, s32[]{:S(2)}) async-start(s8[11796480]{0:T(1024)(128)(4,1)} %bitcast.31), calls=%async_computation | async-start | bytes 8388608
  114.1 24.6 %copy-start.10 = (bf16[32,4608]{1,0:T(8,128)(2,1)}, bf16[32,4608]{1,0:T(8,128)(2,1)S(1)}, u32[]{:S(2)}) copy-start(bf16[32,4608]{1,0:T(8,128)(2,1)S(1)} %get-tuple-element.11) | copy-start | bytes 884740
  138.7 4.4 %copy-start.2 = (f32[2304,1280]{1,0:T(8,128)S(1)}, f32[2304,1280]{1,0:T(8,128)}, u32[]{:S(2)}) copy-start(f32[2304,1280]{1,0:T(8,128)} %weight_ref.6) | copy-start | bytes 35389444
  143.0 5.5 %slice-start.1 = ((s8[11796480]{0:T(1024)(128)(4,1)}), s8[4194304]{0:T(1024)(128)(4,1)S(1)}, s32[]{:S(2)}) async-start(s8[11796480]{0:T(1024)(128)(4,1)} %bitcast.31), calls=%async_computation.1 | async-start | bytes 8388608
  143.0 5.5 %slice-start.2 = ((s8[11796480]{0:T(1024)(128)(4,1)}), s8[3407872]{0:T(1024)(128)(4,1)S(1)}, s32[]{:S(2)}) async-start(s8[11796480]{0:T(1024)(128)(4,1)} %bitcast.31), calls=%async_computation.2 | async-start | bytes 6815744
  154.0 40.4 %collective-permute-start.2 = (bf16[512,1280]{1,0:T(8,128)(2,1)}, bf16[512,1280]{1,0:T(8,128)(2,1)S(1)}, u32[]{:S(2)}, u32[]{:S(2)}) collective-permute-start(bf16[512,1280]{1,0:T(8,128)(2,1)} %shard_map.143), channel_id=1, source_target_pairs={{0,16},{16,0},{1,17},{17,1},{2,18},{18,2},{3,19},{19,3},{4,20},{20... | collective-permute-start | bytes 3932168 | tf_op jit(solution)/shard_map/ppermute | solution.py:155
  154.7 58.6 %collective-permute-start.1 = (bf16[512,1280]{1,0:T(8,128)(2,1)}, bf16[512,1280]{1,0:T(8,128)(2,1)S(1)}, u32[]{:S(2)}, u32[]{:S(2)}) collective-permute-start(bf16[512,1280]{1,0:T(8,128)(2,1)} %shard_map.142), channel_id=1, source_target_pairs={{0,16},{16,0},{1,17},{17,1},{2,18},{18,2},{3,19},{19,3},{4,20},{20... | collective-permute-start | bytes 3932168 | tf_op jit(solution)/shard_map/ppermute | solution.py:155
  180.5 1.5 copy-start.4
  182.0 1.4 copy-start.5
  183.5 4.4 %copy-start.3 = (f32[2304,1280]{1,0:T(8,128)S(1)}, f32[2304,1280]{1,0:T(8,128)}, u32[]{:S(2)}) copy-start(f32[2304,1280]{1,0:T(8,128)} %weight_ref.6) | copy-start | bytes 35389444
  187.8 1.7 copy-start.6
  189.5 27.9 %copy-start.1 = (bf16[256,4608]{1,0:T(8,128)(2,1)S(1)}, bf16[256,4608]{1,0:T(8,128)(2,1)}, u32[]{:S(2)}) copy-start(bf16[256,4608]{1,0:T(8,128)(2,1)} %param.17) | copy-start | bytes 7077892
